TPU v7x, 128 devices: a whole 4x4x4 slice. The times are simulated.
128 devices in a mesh: dp: 2 (over x_lo), lat: 4 (over y), lon: 16 (over x_hi, z, core).
Axes of the slice: x: 4 (x_hi: 2, x_lo: 2; x = x_hi * 2 + x_lo), y: 4, z: 4, core: 2. Of those that a mesh axis runs over, the one named last changes fastest.
Arguments:
- inputs: bfloat16 [2, 128, 256, 1024], P('dp', 'lat', 'lon'), may hold values from -40 to 40
- grad_out: bfloat16 [2, 128, 256, 1024], P('dp', 'lat', 'lon'), may hold values from -6 to 6
- w_qkv: bfloat16 [1024, 3072], replicated, may hold values from -0.1875 to 0.1875
Outputs:
- grad_inputs: bfloat16 [2, 128, 256, 1024], P('dp', 'lat', 'lon')
- grad_w_qkv: float32 [1024, 3072], P(('dp', 'lat', 'lon'))
All inputs are finite; a program needn't handle non-finite values.
Results may differ from a plain program's by a relative error of at most 0.011.
Values may be sent and summed in bfloat16 or wider, within the bound.
A program may use at most 192 MiB of HBM per device.

v0:
```python
import jax
import jax.numpy as jnp
from jax import lax
from jax.sharding import PartitionSpec as P

HEADS = 16
WIN = 13
TILE_R = 8
TILE_C = 16
GROUP = 4


def with_halo(array, sides, width, wrap):
    for axis, dim in sides:
        size, length = (lax.axis_size(axis), array.shape[dim])
        up = [(i, (i + 1) % size) for i in range(size if wrap else size - 1)]
        down = [(j, i) for i, j in up]
        last = lax.slice_in_dim(array, length - width, length, axis=dim)
        leading = lax.slice_in_dim(array, 0, width, axis=dim)
        before = lax.ppermute(last, axis, up)
        after = lax.ppermute(leading, axis, down)
        array = jnp.concatenate([before, array, after], axis=dim)
    return array


def passed_along(block, axis, distance):
    devices = range(lax.axis_size(axis))
    route = [(i - distance, i) for i in devices if i - distance in devices]
    return lax.ppermute(block, axis, route)


def from_behind(array, axis, by):
    size = lax.axis_size(axis)
    return lax.ppermute(array, axis, [(i, (i + by) % size) for i in range(size)])


def tile_layout(row_tile, band_start, band_rows, total_rows):
    margin = WIN // 2
    first_row = band_start + row_tile * TILE_R
    window_top = jnp.clip(first_row - margin, 0, total_rows - WIN)
    region_top = jnp.minimum(window_top - band_start + margin, band_rows - TILE_R)
    query_rows = first_row + jnp.arange(TILE_R, dtype=jnp.int32)
    key_rows = region_top + band_start - margin + jnp.arange(TILE_R + WIN - 1, dtype=jnp.int32)
    return (region_top, query_rows, key_rows)


def window_mask(query_rows, key_rows, total_rows):
    margin = WIN // 2
    starts = jnp.clip(query_rows - margin, 0, total_rows - WIN)
    row_inside = (key_rows[:, None] >= starts[None, :]) & (
        key_rows[:, None] <= starts[None, :] + WIN - 1
    )
    query_cols = jnp.arange(TILE_C, dtype=jnp.int32)
    key_cols = jnp.arange(TILE_C + WIN - 1, dtype=jnp.int32)
    col_inside = (key_cols[:, None] >= query_cols[None, :]) & (
        key_cols[:, None] <= query_cols[None, :] + WIN - 1
    )
    inside = row_inside[:, None, :, None] & col_inside[None, :, None, :]
    return inside.reshape((TILE_R + WIN - 1) * (TILE_C + WIN - 1), TILE_R * TILE_C)


def tile_grads(query_tile, grad_tile, region, inside):
    query_count, width = query_tile.shape
    key_count = region.shape[0]
    head_width = width // HEADS
    norm_scale = head_width ** (-0.5)
    head_queries = query_tile.reshape(query_count, HEADS, head_width)
    head_grads = grad_tile.reshape(query_count, HEADS, head_width)
    head_keys = region[:, :width].reshape(key_count, HEADS, head_width)
    head_values = region[:, width:].reshape(key_count, HEADS, head_width)
    scores = (
        jnp.einsum("khd,ihd->hki", head_keys, head_queries, preferred_element_type=jnp.float32)
        * norm_scale
    )
    scores = jnp.where(inside[None], scores, -1e30)
    maxima = jnp.max(scores, axis=1, keepdims=True)
    exponent = jnp.exp(scores - maxima)
    attn_weights = exponent / jnp.sum(exponent, axis=1, keepdims=True)
    attn_rounded = attn_weights.astype(jnp.bfloat16)
    value_dots = jnp.einsum(
        "khd,ihd->hki", head_values, head_grads, preferred_element_type=jnp.float32
    )
    delta_terms = jnp.sum(attn_weights * value_dots, axis=1, keepdims=True)
    score_grads = (attn_weights * (value_dots - delta_terms)).astype(jnp.bfloat16)
    query_grad = (
        jnp.einsum("hki,khd->ihd", score_grads, head_keys, preferred_element_type=jnp.float32)
        * norm_scale
    )
    key_grad = (
        jnp.einsum("hki,ihd->khd", score_grads, head_queries, preferred_element_type=jnp.float32)
        * norm_scale
    )
    value_grad = jnp.einsum(
        "hki,ihd->khd", attn_rounded, head_grads, preferred_element_type=jnp.float32
    )
    region_grad = jnp.concatenate(
        [key_grad.reshape(key_count, width), value_grad.reshape(key_count, width)], axis=1
    )
    return (query_grad.reshape(query_count, width), region_grad)


def run_tiles(queries, grad_out, key_values, band_start, total_rows):
    samples, band_rows, band_cols, width = queries.shape
    region_rows = TILE_R + WIN - 1
    region_cols = TILE_C + WIN - 1
    row_tiles = band_rows // TILE_R
    col_tiles = band_cols // TILE_C
    tile_count = samples * row_tiles * col_tiles
    anchor = jnp.zeros((), jnp.int32)

    def one_tile(tile_index):
        sample = tile_index // (row_tiles * col_tiles)
        row_tile = tile_index // col_tiles % row_tiles
        col_tile = tile_index % col_tiles
        region_top, query_rows, key_rows = tile_layout(row_tile, band_start, band_rows, total_rows)
        first_col = col_tile * TILE_C
        query_tile = lax.dynamic_slice(
            queries, (sample, row_tile * TILE_R, first_col, anchor), (1, TILE_R, TILE_C, width)
        ).reshape(TILE_R * TILE_C, width)
        grad_tile = lax.dynamic_slice(
            grad_out, (sample, row_tile * TILE_R, first_col, anchor), (1, TILE_R, TILE_C, width)
        ).reshape(TILE_R * TILE_C, width)
        region = lax.dynamic_slice(
            key_values,
            (sample, region_top, first_col, anchor),
            (1, region_rows, region_cols, 2 * width),
        ).reshape(region_rows * region_cols, 2 * width)
        query_grad, region_grad = tile_grads(
            query_tile, grad_tile, region, window_mask(query_rows, key_rows, total_rows)
        )
        return (query_grad, region_grad, sample, region_top, first_col)

    def group_step(totals, group_index):
        tile_ids = group_index * GROUP + jnp.arange(GROUP, dtype=jnp.int32)
        query_grads, region_grads, sample_ids, region_tops, region_lefts = jax.vmap(one_tile)(
            tile_ids
        )
        for member in range(GROUP):
            corner = (sample_ids[member], region_tops[member], region_lefts[member], anchor)
            current = lax.dynamic_slice(totals, corner, (1, region_rows, region_cols, 2 * width))
            totals = lax.dynamic_update_slice(
                totals,
                current + region_grads[member].reshape(1, region_rows, region_cols, 2 * width),
                corner,
            )
        return (totals, query_grads)

    initial = jnp.zeros((samples, band_rows + WIN - 1, band_cols + WIN - 1, 2 * width), jnp.float32)
    totals, query_grads = lax.scan(
        group_step, initial, jnp.arange(tile_count // GROUP, dtype=jnp.int32)
    )
    query_grads = query_grads.reshape(samples, row_tiles, col_tiles, TILE_R, TILE_C, width)
    query_grads = query_grads.transpose(0, 1, 3, 2, 4, 5).reshape(
        samples, band_rows, band_cols, width
    )
    return (query_grads, totals)


def along_longitude(tensor):
    return with_halo(tensor, (("lon", 2),), WIN // 2, True)


def along_latitude(tensor):
    return with_halo(tensor, (("lat", 1),), WIN // 2, False)


def extend(tensor):
    widened = along_latitude(along_longitude(tensor))
    return widened


def give_back_latitude(totals):
    margin = WIN // 2
    extent = totals.shape[1]
    for offset in (1, -1):
        outgoing = totals[:, extent - margin :] if offset == 1 else totals[:, :margin]
        incoming = passed_along(outgoing, "lat", offset)
        if offset == 1:
            totals = totals.at[:, margin : 2 * margin].add(incoming)
        else:
            totals = totals.at[:, extent - 2 * margin : extent - margin].add(incoming)
    return totals


def give_back_longitude(totals):
    margin = WIN // 2
    extent = totals.shape[2]
    for offset in (1, -1):
        outgoing = totals[:, :, extent - margin :] if offset == 1 else totals[:, :, :margin]
        incoming = from_behind(outgoing, "lon", offset)
        if offset == 1:
            totals = totals.at[:, :, margin : 2 * margin].add(incoming)
        else:
            totals = totals.at[:, :, extent - 2 * margin : extent - margin].add(incoming)
    return totals


def body(inputs, grad_out, w_qkv):
    samples, band_rows, band_cols, width = inputs.shape
    margin = WIN // 2
    lat_count = lax.axis_size("lat")
    lon_count = lax.axis_size("lon")
    dp_count = lax.axis_size("dp")
    band_start = lax.axis_index("lat") * band_rows
    total_rows = band_rows * lat_count
    flat_inputs = inputs.reshape(-1, width)
    projected = jnp.dot(flat_inputs, w_qkv, preferred_element_type=jnp.float32).astype(jnp.bfloat16)
    projected = projected.reshape(samples, band_rows, band_cols, 3 * width)
    queries = projected[..., :width]
    key_values = extend(projected[..., width:])
    query_grads, totals = run_tiles(queries, grad_out, key_values, band_start, total_rows)
    totals = give_back_latitude(totals)[:, margin : band_rows + margin]
    totals = give_back_longitude(totals)[:, :, margin : band_cols + margin]
    grad_proj = jnp.concatenate(
        [query_grads.astype(jnp.bfloat16), totals.astype(jnp.bfloat16)], axis=-1
    ).reshape(-1, 3 * width)
    grad_inputs = lax.dot_general(
        grad_proj, w_qkv, (((1,), (1,)), ((), ())), preferred_element_type=jnp.float32
    )
    grad_inputs = grad_inputs.astype(jnp.bfloat16).reshape(inputs.shape)
    devices_all = dp_count * lat_count * lon_count
    grad_scale = float(samples * band_rows * band_cols * devices_all) ** (-0.5)
    grad_w_qkv = lax.psum_scatter(
        lax.dot_general(
            flat_inputs, grad_proj, (((0,), (0,)), ((), ())), preferred_element_type=jnp.float32
        )
        * grad_scale,
        ("dp", "lat", "lon"),
        scatter_dimension=0,
        tiled=True,
    )
    return (grad_inputs, grad_w_qkv)


def solution(mesh):
    in_specs = (P("dp", "lat", "lon", None), P("dp", "lat", "lon", None), P())
    out_specs = (P("dp", "lat", "lon", None), P(("dp", "lat", "lon"), None))
    return jax.shard_map(body, mesh=mesh, in_specs=in_specs, out_specs=out_specs, check_vma=False)
```

profile of v0, /device:TPU:0, one launch (start us, length us, event | category | flops | bytes accessed | tf_op | source)
XLA Modules:
  0.0 1234.7 jit_solution(6444346213126525184)
XLA Ops:
  8.4 6.4 convolution_convert_fusion
  79.7 6.1 pad_maximum_fusion
  85.8 19.4 %while.10 = (s32[]{:T(128)}, bf16[1,44,28,2048]{3,2,1,0:T(8,128)(2,1)}, s32[4,4]{1,0:T(4,128)S(1)}, bf16[4,1,20,28,2048]{4,3,2,1,0:T(8,128)(2,1)}, s32[]{:T(128)}) while((s32[]{:T(128)}, bf16[1,44,28,2048]{3,2,1,0:T(8,128)(2,1)}, s32[4,4]{1,0:T(4,128)S(1)}, bf16[4,1,20,28,2048]{4,3,2,1,0:T(8,128)(2,1)}, s32[]{:T(128)}) %tuple.55), condition=%wide.while_cond.4, body=%wide.while_body.4.sunk | while | flops 2 | bytes 5244009 | solution.py:123
  105.2 12.1 copy.42
  117.4 10.3 fusion.45
  127.7 9.5 copy.43
  137.2 9.6 copy.47
  146.7 12.6 %fusion.48 = (f32[4,16,128]{2,1,0:T(8,128)S(1)}, f32[4,16,560,128]{3,2,1,0:T(8,128)}) fusion(pred[4,560,128]{2,1,0:T(8,128)(4,1)S(1)} %copy-done.9, bf16[4,560,16,64]{1,3,2,0:T(8,128)(2,1)} %bitcast.76, bf16[4,128,16,64]{1,3,2,0:T(8,128)(2,1)S(1)} %copy-done.7), kind=kOutput, calls=%fused_computation.97 | convolution fusion | flops 605553216 | bytes 24305664 | tf_op jit(solution)/shard_map/while/body/eval_jaxpr/vmap()/sub | solution.py:77
  159.3 13.6 %fusion.3 = f32[4,16,64,560]{3,2,1,0:T(8,128)} fusion(bf16[4,128,16,64]{1,3,2,0:T(8,128)(2,1)S(1)} %copy-done.8, f32[4,16,560,128]{3,2,1,0:T(8,128)} %get-tuple-element.110, f32[4,16,128]{2,1,0:T(8,128)S(1)} %get-tuple-element.109), kind=kOutput, calls=%fused_computation.18 | convolution fusion | flops 596377600 | bytes 28606464 | tf_op jit(solution)/shard_map/while/body/eval_jaxpr/vmap(hki,ihd->khd)/dot_general | solution.py:93
  172.8 14.2 %multiply_reduce_fusion = (f32[4,16,128]{2,1,0:T(8,128)S(1)}, f32[4,16,560,128]{3,2,1,0:T(8,128)}) fusion(f32[4,16,560,128]{3,2,1,0:T(8,128)} %get-tuple-element.110, f32[4,16,128]{2,1,0:T(8,128)S(1)} %get-tuple-element.109, bf16[4,560,16,64]{1,3,2,0:T(8,128)(2,1)} %bitcast.88, bf16[4,128,16,64]{1,3,2,0:T(8,128)(2,1)S(1)} %copy-done.8), kind=kOutput, calls=%fused_computation.12 | convolution fusion | flops 600956928 | bytes 42401792 | tf_op jit(solution)/shard_map/while/body/eval_jaxpr/vmap(khd,ihd->hki)/dot_general | solution.py:80
  187.0 12.6 %multiply_convert_fusion = bf16[4,16,560,128]{3,2,1,0:T(8,128)(2,1)S(1)} fusion(f32[4,16,560,128]{3,2,1,0:T(8,128)} %get-tuple-element.112, f32[4,16,128]{2,1,0:T(8,128)S(1)} %get-tuple-element.111, f32[4,16,560,128]{3,2,1,0:T(8,128)} %get-tuple-element.110, f32[4,16,128]{2,1,0:T(8,128)S(1)} %get-tuple-element.109), kind=kLoop, calls=%fused_computation.11 | loop fusion | flops 18350080 | bytes 45940736 | tf_op jit(solution)/shard_map/while/body/eval_jaxpr/vmap()/convert_element_type | solution.py:84
  199.6 6.6 broadcast_multiply_fusion
  206.4 12.6 %copy.53 = f32[4,560,1024]{2,0,1:T(4,128)} copy(f32[4,560,1024]{1,2,0:T(8,128)} %bitcast.74) | data formatting | bytes 18350080 | tf_op jit(solution)/shard_map/while/body/eval_jaxpr/vmap()/reshape | solution.py:97
  219.0 12.7 %copy.54 = f32[4,560,1024]{2,0,1:T(4,128)} copy(f32[4,560,1024]{1,2,0:T(8,128)} %bitcast.84) | data formatting | bytes 18350080 | tf_op jit(solution)/shard_map/while/body/eval_jaxpr/vmap()/reshape | solution.py:97
  231.7 44.8 %pad_maximum_fusion.1 = (f32[1,560,2048]{2,0,1:T(1,128)}, f32[1,560,2048]{2,0,1:T(1,128)S(1)}, f32[1,560,2048]{2,0,1:T(1,128)}, f32[1,560,2048]{2,0,1:T(1,128)}) fusion(f32[4,560,1024]{2,0,1:T(4,128)} %copy.54, f32[4,560,1024]{2,0,1:T(4,128)} %copy.53), kind=kLoop, calls=%fused_computation.32 | loop fusion | flops 4587520 | bytes 36700160 | tf_op jit(solution)/shard_map/while/body/eval_jaxpr/vmap()/concatenate | solution.py:96
  287.2 20.9 %dynamic_update_slice.23 = f32[1,44,28,2048]{3,1,2,0:T(8,128)} dynamic-update-slice(f32[1,44,28,2048]{3,1,2,0:T(8,128)} %broadcast_in_dim.69, f32[1,20,28,2048]{3,1,2,0:T(8,128)} %copy.55, s32[]{:T(128)} %constant.235.clone.1, s32[]{:T(128)S(6)} %select_n.168, s32[]{:T(128)} %constant.235.clone.1, s32[]{:T(128)} %constant.235.clone.1) | dynamic-update-slice | bytes 9175044 | tf_op jit(solution)/shard_map/while/body/eval_jaxpr/dynamic_update_slice | solution.py:141
  308.1 10.1 copy_add_fusion.2
  318.2 20.6 %dynamic_update_slice.24 = f32[1,44,28,2048]{3,1,2,0:T(8,128)} dynamic-update-slice(f32[1,44,28,2048]{3,1,2,0:T(8,128)} %dynamic_update_slice.23, f32[1,20,28,2048]{3,1,2,0:T(8,128)} %copy_add_fusion.2, s32[]{:T(128)} %constant.235.clone.1, s32[]{:T(128)S(6)} %select_n.169, s32[]{:T(128)} %constant.235.clone.1, s32[]{:T(128)} %constant.235.clone.1) | dynamic-update-slice | bytes 9175044 | tf_op jit(solution)/shard_map/while/body/eval_jaxpr/dynamic_update_slice | solution.py:141
  338.8 10.1 copy_add_fusion.1
  348.9 20.2 %dynamic_update_slice.25 = f32[1,44,28,2048]{3,1,2,0:T(8,128)} dynamic-update-slice(f32[1,44,28,2048]{3,1,2,0:T(8,128)} %dynamic_update_slice.24, f32[1,20,28,2048]{3,1,2,0:T(8,128)} %copy_add_fusion.1, s32[]{:T(128)} %constant.235.clone.1, s32[]{:T(128)S(6)} %select_n.170, s32[]{:T(128)} %constant.235.clone.1, s32[]{:T(128)} %constant.235.clone.1) | dynamic-update-slice | bytes 9175044 | tf_op jit(solution)/shard_map/while/body/eval_jaxpr/dynamic_update_slice | solution.py:141
  369.0 9.6 copy_add_fusion
  378.6 19.7 %dynamic_update_slice.26 = f32[1,44,28,2048]{3,1,2,0:T(8,128)} dynamic-update-slice(f32[1,44,28,2048]{3,1,2,0:T(8,128)} %dynamic_update_slice.25, f32[1,20,28,2048]{3,1,2,0:T(8,128)} %copy_add_fusion, s32[]{:T(128)} %constant.235.clone.1, s32[]{:T(128)S(6)} %select_n.171, s32[]{:T(128)} %constant.235.clone.1, s32[]{:T(128)} %constant.235.clone.1) | dynamic-update-slice | bytes 9175044 | tf_op jit(solution)/shard_map/while/body/eval_jaxpr/dynamic_update_slice | solution.py:141
  406.4 25.0 %collective-permute-done.4 = f32[1,6,28,2048]{3,0,2,1:T(1,128)S(1)} collective-permute-done((f32[1,6,28,2048]{3,0,2,1:T(1,128)S(1)}, f32[1,6,28,2048]{3,0,2,1:T(1,128)S(1)}, u32[]{:S(2)}, u32[]{:S(2)}) %collective-permute-start.4) | collective-permute-done | bytes 1376288 | tf_op jit(solution)/shard_map/ppermute | solution.py:29
  434.6 9.5 scatter-add.14
  448.5 28.0 %collective-permute-done.5 = f32[1,6,28,2048]{3,0,2,1:T(1,128)S(1)} collective-permute-done((f32[1,6,28,2048]{3,0,2,1:T(1,128)S(1)}, f32[1,6,28,2048]{3,0,2,1:T(1,128)S(1)}, u32[]{:S(2)}, u32[]{:S(2)}) %collective-permute-start.5) | collective-permute-done | bytes 1376288 | tf_op jit(solution)/shard_map/ppermute | solution.py:29
  480.3 10.0 scatter-add.15
  496.9 18.6 %collective-permute-done.6 = f32[1,32,6,2048]{3,1,2,0:T(8,128)S(1)} collective-permute-done((f32[1,32,6,2048]{3,1,2,0:T(8,128)S(1)}, f32[1,32,6,2048]{3,1,2,0:T(8,128)S(1)}, u32[]{:S(2)}, u32[]{:S(2)}) %collective-permute-start.6) | collective-permute-done | bytes 1572896 | tf_op jit(solution)/shard_map/ppermute | solution.py:34
  531.7 8.1 collective-permute-done.7
  547.1 7.7 fusion.2
  554.8 12.6 %copy.70 = f32[1024,3072]{1,0:T(8,128)} copy(f32[1024,3072]{0,1:T(8,128)} %fusion.2) | data formatting | bytes 25165824
  572.4 7.6 fusion.19
  580.0 647.6 %reduce-scatter.4.cloned.1.call-done = f32[8,3072]{1,0:T(8,128)} async-done(((f32[1024,3072]{1,0:T(8,128)}), f32[8,3072]{1,0:T(8,128)}) %reduce-scatter.4.cloned.1.call-update) | async-done | bytes 98320
  (111 shorter events, 143.1 us)
Async XLA Ops:
  7.2 1.2 copy-start
  7.2 1220.4 %reduce-scatter.4.cloned.1.call-start = ((), (), s32[]{:S(2)}) async-start(), calls=%async_computation.1 | async-start | bytes 12681216
  14.8 1.8 copy-start.5
  18.3 20.9 %collective-permute-start = (bf16[1,32,6,2048]{3,1,2,0:T(8,128)(2,1)}, bf16[1,32,6,2048]{3,1,2,0:T(8,128)(2,1)}, u32[]{:S(2)}, u32[]{:S(2)}) collective-permute-start(bf16[1,32,6,2048]{3,1,2,0:T(8,128)(2,1)} %copy.73), channel_id=1, source_target_pairs={{0,1},{1,2},{2,3},{3,4},{4,5},{5,6},{6,7},{7,8},{8,9},{9,10},{10,1... | collective-permute-start | bytes 2359304 | tf_op jit(solution)/shard_map/ppermute | solution.py:20
  19.6 21.1 %collective-permute-start.1 = (bf16[1,32,6,2048]{3,1,2,0:T(8,128)(2,1)}, bf16[1,32,6,2048]{3,1,2,0:T(8,128)(2,1)}, u32[]{:S(2)}, u32[]{:S(2)}) collective-permute-start(bf16[1,32,6,2048]{3,1,2,0:T(8,128)(2,1)} %copy.74), channel_id=1, source_target_pairs={{1,0},{2,1},{3,2},{4,3},{5,4},{6,5},{7,6},{8,7},{9,8},{10,9},{11,1... | collective-permute-start | bytes 2359304 | tf_op jit(solution)/shard_map/ppermute | solution.py:21
  40.7 2.0 copy-start.3
  42.7 1.8 copy-start.4
  44.4 35.3 %collective-permute-start.2 = (bf16[1,6,28,2048]{3,2,1,0:T(8,128)(2,1)}, bf16[1,6,28,2048]{3,2,1,0:T(8,128)(2,1)}, u32[]{:S(2)}, u32[]{:S(2)}) collective-permute-start(bf16[1,6,28,2048]{3,2,1,0:T(8,128)(2,1)} %get-tuple-element.99), channel_id=1, source_target_pairs={{0,16},{16,32},{32,48},{1,17},{17,33},{33,49},{2,18},{18,34},{34,5... | collective-permute-start | bytes 2064392 | tf_op jit(solution)/shard_map/ppermute | solution.py:20
  48.8 30.9 %collective-permute-start.3 = (bf16[1,6,28,2048]{3,2,1,0:T(8,128)(2,1)}, bf16[1,6,28,2048]{3,2,1,0:T(8,128)(2,1)}, u32[]{:S(2)}, u32[]{:S(2)}) collective-permute-start(bf16[1,6,28,2048]{3,2,1,0:T(8,128)(2,1)} %get-tuple-element.100), channel_id=1, source_target_pairs={{16,0},{32,16},{48,32},{17,1},{33,17},{49,33},{18,2},{34,18},{50,3... | collective-permute-start | bytes 2064392 | tf_op jit(solution)/shard_map/ppermute | solution.py:21
  137.2 9.6 copy-start.7
  137.2 9.6 copy-start.9
  146.7 12.6 %copy-start.8 = (bf16[4,128,16,64]{1,3,2,0:T(8,128)(2,1)S(1)}, bf16[4,128,16,64]{1,3,2,0:T(8,128)(2,1)}, u32[]{:S(2)}) copy-start(bf16[4,128,16,64]{1,3,2,0:T(8,128)(2,1)} %copy.49) | copy-start | bytes 3145732
  199.6 6.8 copy-start.1
  402.0 29.5 %collective-permute-start.4 = (f32[1,6,28,2048]{3,0,2,1:T(1,128)S(1)}, f32[1,6,28,2048]{3,0,2,1:T(1,128)S(1)}, u32[]{:S(2)}, u32[]{:S(2)}) collective-permute-start(f32[1,6,28,2048]{3,0,2,1:T(1,128)S(1)} %copy.59), channel_id=1, source_target_pairs={{0,16},{16,32},{32,48},{1,17},{17,33},{33,49},{2,18},{18,34},{34,5... | collective-permute-start | bytes 4128776 | tf_op jit(solution)/shard_map/ppermute | solution.py:29
  447.2 29.3 %collective-permute-start.5 = (f32[1,6,28,2048]{3,0,2,1:T(1,128)S(1)}, f32[1,6,28,2048]{3,0,2,1:T(1,128)S(1)}, u32[]{:S(2)}, u32[]{:S(2)}) collective-permute-start(f32[1,6,28,2048]{3,0,2,1:T(1,128)S(1)} %copy.61), channel_id=1, source_target_pairs={{16,0},{32,16},{48,32},{17,1},{33,17},{49,33},{18,2},{34,18},{50,3... | collective-permute-start | bytes 4128776 | tf_op jit(solution)/shard_map/ppermute | solution.py:29
  480.3 41.3 %slice-start.3 = ((s8[5242880]{0:T(1024)(128)(4,1)}), s8[1048576]{0:T(1024)(128)(4,1)S(1)}, s32[]{:S(2)}) async-start(s8[5242880]{0:T(1024)(128)(4,1)} %bitcast.77), calls=%async_computation.5 | async-start | bytes 2097152
  492.0 29.6 %slice-start.4 = ((s8[5242880]{0:T(1024)(128)(4,1)}), s8[4194304]{0:T(1024)(128)(4,1)S(1)}, s32[]{:S(2)}) async-start(s8[5242880]{0:T(1024)(128)(4,1)} %bitcast.77), calls=%async_computation.6 | async-start | bytes 8388608
  492.0 23.5 %collective-permute-start.6 = (f32[1,32,6,2048]{3,1,2,0:T(8,128)S(1)}, f32[1,32,6,2048]{3,1,2,0:T(8,128)S(1)}, u32[]{:S(2)}, u32[]{:S(2)}) collective-permute-start(f32[1,32,6,2048]{3,1,2,0:T(8,128)S(1)} %slice.284), channel_id=1, source_target_pairs={{0,1},{1,2},{2,3},{3,4},{4,5},{5,6},{6,7},{7,8},{8,9},{9,10},{10,1... | collective-permute-start | bytes 4718600 | tf_op jit(solution)/shard_map/ppermute | solution.py:34
  492.1 29.5 %slice-start = ((s8[9175040]{0:T(1024)(128)(4,1)}), s8[4194304]{0:T(1024)(128)(4,1)S(1)}, s32[]{:S(2)}) async-start(s8[9175040]{0:T(1024)(128)(4,1)} %bitcast.72), calls=%async_computation.2 | async-start | bytes 8388608
  492.1 29.5 %slice-start.1 = ((s8[9175040]{0:T(1024)(128)(4,1)}), s8[786432]{0:T(1024)(128)(4,1)S(1)}, s32[]{:S(2)}) async-start(s8[9175040]{0:T(1024)(128)(4,1)} %bitcast.72), calls=%async_computation.3 | async-start | bytes 1572864
  496.9 24.7 %slice-start.2 = ((s8[9175040]{0:T(1024)(128)(4,1)}), s8[4194304]{0:T(1024)(128)(4,1)S(1)}, s32[]{:S(2)}) async-start(s8[9175040]{0:T(1024)(128)(4,1)} %bitcast.72), calls=%async_computation.4 | async-start | bytes 8388608
  517.4 2.9 copy-start.2
  521.6 18.3 %collective-permute-start.7 = (f32[1,32,6,2048]{3,1,2,0:T(8,128)}, f32[1,32,6,2048]{3,1,2,0:T(8,128)}, u32[]{:S(2)}, u32[]{:S(2)}) collective-permute-start(f32[1,32,6,2048]{3,1,2,0:T(8,128)} %slice.286), channel_id=1, source_target_pairs={{0,15},{1,0},{2,1},{3,2},{4,3},{5,4},{6,5},{7,6},{8,7},{9,8},{10,9... | collective-permute-start | bytes 4718600 | tf_op jit(solution)/shard_map/ppermute | solution.py:34
  545.7 1.4 copy-start.6
Sparse Core Ops, SparseCore 0:
  567.5 660.0 reduce-scatter.3
where the time goes:
time: 1250 us; the launch traced here: 1230 us
  waiting for transfers between devices  727 us (58%)
  local copies, waits for them, and re-layouts  287 us (23%)
  other arithmetic  109 us (9%)
  matrix products  71.7 us (6%)
  between operations  22.1 us (2%)
  starting transfers between devices  17.7 us (1%)
    unnamed x2, waiting for transfers between devices  648 us
    dynamic_update_slice x4, local copies, waits for them, and re-layouts, group_step(): lax.dynamic_update_slice(totals, current + region_grads[member].reshape(1...  81.3 us
    ppermute x2, waiting for transfers between devices, passed_along(): return lax.ppermute(block, axis, route)  53.1 us
    concatenate x1, other arithmetic, tile_grads(): jnp.concatenate([key_grad.reshape(key_count, width), value_grad.reshape(k...  44.8 us
    add x3, other arithmetic, group_step(): current + region_grads[member].reshape(1, region_rows, region_cols, 2 * w...  29.8 us
    ppermute x2, waiting for transfers between devices, from_behind(): lax.ppermute(array, axis, [(i, (i + by) % size) for i in range(size)])  26.8 us
  transfers between devices with their start and end apart: 9, of which 5 were waited for; matrix products, arithmetic and copies ran while one was open for 5% of the time, Pallas kernels for 0%

commit v1 on v0

v1 whole, which is shorter than its diff:
```python
import functools

import jax
import jax.numpy as jnp
from jax import lax
from jax.experimental import pallas as pl
from jax.experimental.pallas import tpu as pltpu
from jax.sharding import PartitionSpec as P

WIN = 13
MARGIN = WIN // 2
HEAD = 64
QUAD = 4
WIDTH = QUAD * HEAD
LAT_DEV = 32
LON_DEV = 16
ROW_T = 4
TILES = LAT_DEV // ROW_T
QUERIES = ROW_T * LON_DEV
KEY_ROWS = ROW_T + WIN - 1
SIDE = 2 * MARGIN
KEYS_A = KEY_ROWS * LON_DEV
KEYS_B = KEY_ROWS * SIDE
KEYS = KEYS_A + KEYS_B
PAD_ROWS = 2
OWN = (PAD_ROWS + MARGIN) * LON_DEV
OWN_N = LAT_DEV * LON_DEV
SPLIT = (PAD_ROWS + LAT_DEV + SIDE) * LON_DEV
TOKENS = 1280
D = 1024
NT = (((1,), (1,)), ((), ()))
TN = (((0,), (0,)), ((), ()))
NN = (((1,), (0,)), ((), ()))
MESH = pl.DeviceIdType.MESH


def mm(a, b, dims=NN):
    return lax.dot_general(a, b, dims, preferred_element_type=jnp.float32)


def key_tile(t, first_band, last_band):
    lead = jnp.logical_and(first_band, t == 0).astype(jnp.int32)
    tail = jnp.logical_and(last_band, t == TILES - 1).astype(jnp.int32)
    return t + lead - tail


def window_bias(t, top, keys, side, band_start, total_rows):
    kk = lax.broadcasted_iota(jnp.int32, (keys, WIDTH), 0)
    qq = lax.broadcasted_iota(jnp.int32, (keys, WIDTH), 1) & (QUERIES - 1)
    i, j = qq >> 4, qq & 15
    if side:
        r = (kk * 171) >> 11
        c = kk - r * SIDE
        col = jnp.where(c < MARGIN, c - MARGIN, c + (LON_DEV - MARGIN))
    else:
        r, col = kk >> 4, kk & 15
    first = band_start + ROW_T * t
    key_row = band_start + ROW_T * top - MARGIN + r
    start = jnp.clip(first + i - MARGIN, 0, total_rows - WIN)
    off = key_row - start
    away = col - j
    inside = (off >= 0) & (off < WIN) & (away >= -MARGIN) & (away <= MARGIN)
    return jnp.where(inside, 0.0, -1e30).astype(jnp.float32)


def spread(tile, same_head):
    return jnp.concatenate([tile] * QUAD, axis=0) * same_head


def attend(t, top, q, k, v, go, bias, same, dk, dv, dq):
    own = pl.ds(t * QUERIES, QUERIES)
    ka = pl.ds(pl.multiple_of(PAD_ROWS * LON_DEV + top * QUERIES, 32), KEYS_A)
    kb = pl.ds(pl.multiple_of(SPLIT + top * ROW_T * SIDE, 16), KEYS_B)
    same_head = same[...]
    bq = spread(q[own, :], same_head)
    bg = spread(go[own, :], same_head)
    sa = mm(k[ka, :], bq, NT) + bias[t, :KEYS_A, :]
    sb = mm(k[kb, :], bq, NT) + bias[t, KEYS_A:, :]
    peak = jnp.maximum(jnp.max(sa, axis=0, keepdims=True), jnp.max(sb, axis=0, keepdims=True))
    pa = jnp.exp(sa - peak)
    pb = jnp.exp(sb - peak)
    da = mm(v[ka, :], bg, NT)
    db = mm(v[kb, :], bg, NT)
    inv = 1.0 / (jnp.sum(pa, axis=0, keepdims=True) + jnp.sum(pb, axis=0, keepdims=True))
    delta = (
        jnp.sum(pa * da, axis=0, keepdims=True) + jnp.sum(pb * db, axis=0, keepdims=True)
    ) * inv
    pa = pa * inv
    pb = pb * inv
    aa = pa.astype(jnp.bfloat16)
    ab = pb.astype(jnp.bfloat16)
    ea = (pa * (da - delta)).astype(jnp.bfloat16)
    eb = (pb * (db - delta)).astype(jnp.bfloat16)
    dk[ka, :] += mm(ea, bq)
    dk[kb, :] += mm(eb, bq)
    dv[ka, :] += mm(aa, bg)
    dv[kb, :] += mm(ab, bg)
    mixed = (mm(ea, k[ka, :], TN) + mm(eb, k[kb, :], TN)) * same_head.astype(jnp.float32)
    total = mixed[:QUERIES]
    for h in range(1, QUAD):
        total = total + mixed[h * QUERIES : (h + 1) * QUERIES]
    dq[own, :] = (total * HEAD**-0.5).astype(jnp.bfloat16)


def feature_order(block):
    row = lax.broadcasted_iota(jnp.int32, (256, D), 0) + block * 256
    col = lax.broadcasted_iota(jnp.int32, (256, D), 1)
    r = row & 7
    xlo = (row >> 3) & 1
    xhi = (row >> 4) & 1
    y = (row >> 5) & 3
    z = (row >> 7) & 3
    core = row >> 9
    source = (((((xlo * 4 + y) * 2 + xhi) * 4 + z) * 2 + core) << 3) + r
    return jnp.where(col == source, 1.0, 0.0).astype(jnp.bfloat16)


def attention_kernel(
    scale, unroll, x, go, wq, wk, wv, gw, gi, q, k, v, dq, dk, dv, bias, same, xt, total
):
    g = pl.program_id(0)
    band_start = lax.axis_index("lat") * LAT_DEV
    total_rows = LAT_DEV * lax.axis_size("lat")
    first_band = lax.axis_index("lat") == 0
    last_band = lax.axis_index("lat") == lax.axis_size("lat") - 1

    @pl.when(g == 0)
    def _():
        @pl.loop(0, TILES)
        def _(t):
            top = key_tile(t, first_band, last_band)
            bias[t, :KEYS_A, :] = window_bias(t, top, KEYS_A, False, band_start, total_rows)
            bias[t, KEYS_A:, :] = window_bias(t, top, KEYS_B, True, band_start, total_rows)

        row = lax.broadcasted_iota(jnp.int32, (WIDTH, WIDTH), 0)
        col = lax.broadcasted_iota(jnp.int32, (WIDTH, WIDTH), 1)
        same[...] = jnp.where((row >> 6) == (col >> 6), 1.0, 0.0).astype(jnp.bfloat16)

        @pl.loop(0, 4)
        def _(b):
            rows = pl.ds(b * 256, 256)
            xt[rows, :] = mm(feature_order(b), x[...], NT).astype(jnp.bfloat16)

    q[...] = (mm(x[OWN : OWN + OWN_N, :], wq[...]).astype(jnp.bfloat16)) * jnp.bfloat16(0.125)
    k[...] = mm(x[...], wk[...]).astype(jnp.bfloat16)
    v[...] = mm(x[...], wv[...]).astype(jnp.bfloat16)
    dk[...] = jnp.zeros_like(dk)
    dv[...] = jnp.zeros_like(dv)
    if unroll == TILES:
        for t in range(TILES):
            attend(t, key_tile(t, first_band, last_band), q, k, v, go, bias, same, dk, dv, dq)
    else:
        @pl.loop(0, TILES, unroll=unroll)
        def _(t):
            attend(t, key_tile(t, first_band, last_band), q, k, v, go, bias, same, dk, dv, dq)
    dkb = dk[...].astype(jnp.bfloat16)
    dvb = dv[...].astype(jnp.bfloat16)
    gw[0, 0] = (mm(xt[:, OWN : OWN + OWN_N], dq[...]) * scale).astype(jnp.bfloat16)
    gw[0, 1] = (mm(xt[...], dkb) * scale).astype(jnp.bfloat16)
    gw[0, 2] = (mm(xt[...], dvb) * scale).astype(jnp.bfloat16)
    part = mm(
        jnp.concatenate([dkb, dvb], axis=1), jnp.concatenate([wk[...], wv[...]], axis=1), NT
    )

    @pl.when(g == 0)
    def _():
        total[...] = part

    @pl.when(g > 0)
    def _():
        total[...] += part

    total[OWN : OWN + OWN_N, :] += mm(dq[...], wq[...], NT)

    @pl.when(g == pl.num_programs(0) - 1)
    def _():
        gi[...] = total[...]


def attention(x, go, w, scale, unroll=2):
    quads = D // WIDTH
    scratch = [
        pltpu.VMEM((OWN_N, WIDTH), jnp.bfloat16),
        pltpu.VMEM((TOKENS, WIDTH), jnp.bfloat16),
        pltpu.VMEM((TOKENS, WIDTH), jnp.bfloat16),
        pltpu.VMEM((OWN_N, WIDTH), jnp.bfloat16),
        pltpu.VMEM((TOKENS, WIDTH), jnp.float32),
        pltpu.VMEM((TOKENS, WIDTH), jnp.float32),
        pltpu.VMEM((TILES, KEYS, WIDTH), jnp.float32),
        pltpu.VMEM((WIDTH, WIDTH), jnp.bfloat16),
        pltpu.VMEM((D, TOKENS), jnp.bfloat16),
        pltpu.VMEM((TOKENS, D), jnp.float32),
    ]
    return pl.pallas_call(
        functools.partial(attention_kernel, scale, unroll),
        grid=(quads,),
        in_specs=[
            pl.BlockSpec((TOKENS, D), lambda g: (0, 0)),
            pl.BlockSpec((OWN_N, WIDTH), lambda g: (0, g)),
            pl.BlockSpec((D, WIDTH), lambda g: (0, g)),
            pl.BlockSpec((D, WIDTH), lambda g: (0, quads + g)),
            pl.BlockSpec((D, WIDTH), lambda g: (0, 2 * quads + g)),
        ],
        out_specs=[
            pl.BlockSpec((1, 3, D, WIDTH), lambda g: (g, 0, 0, 0)),
            pl.BlockSpec((TOKENS, D), lambda g: (0, 0)),
        ],
        out_shape=[
            jax.ShapeDtypeStruct((quads, 3, D, WIDTH), jnp.bfloat16),
            jax.ShapeDtypeStruct((TOKENS, D), jnp.float32),
        ],
        scratch_shapes=scratch,
        compiler_params=pltpu.CompilerParams(vmem_limit_bytes=60 * 2**20),
        name="attention",
    )(x, go, w, w, w)


def shifted(block, axis, by, wrap):
    size = lax.axis_size(axis)
    route = [(i, (i + by) % size) for i in range(size) if wrap or 0 <= i + by < size]
    return lax.ppermute(block, axis, route)


def extended(inputs):
    x = inputs[0]
    above = shifted(x[-MARGIN:], "lat", 1, False)
    below = shifted(x[:MARGIN], "lat", -1, False)
    tall = jnp.concatenate([above, x, below], axis=0)
    left = shifted(tall[:, -MARGIN:], "lon", 1, True)
    right = shifted(tall[:, :MARGIN], "lon", -1, True)
    sides = jnp.concatenate([left, right], axis=1).reshape(-1, D)
    lead = jnp.zeros((PAD_ROWS * LON_DEV, D), x.dtype)
    end = jnp.zeros((TOKENS - SPLIT - sides.shape[0], D), x.dtype)
    return jnp.concatenate([lead, tall.reshape(-1, D), sides, end], axis=0)


def given_back(gi):
    main = gi[PAD_ROWS * LON_DEV : SPLIT].reshape(LAT_DEV + SIDE, LON_DEV, D)
    sides = gi[SPLIT : SPLIT + (LAT_DEV + SIDE) * SIDE].reshape(LAT_DEV + SIDE, SIDE, D)
    sides = sides.astype(jnp.bfloat16)
    from_right = shifted(sides[:, :MARGIN], "lon", -1, True)
    from_left = shifted(sides[:, MARGIN:], "lon", 1, True)
    extra = jnp.concatenate(
        [from_left, jnp.zeros((LAT_DEV + SIDE, LON_DEV - SIDE, D), jnp.bfloat16), from_right], axis=1
    )
    main = main + extra.astype(jnp.float32)
    from_below = shifted(main[:MARGIN].astype(jnp.bfloat16), "lat", -1, False)
    from_above = shifted(main[-MARGIN:].astype(jnp.bfloat16), "lat", 1, False)
    extra = jnp.concatenate(
        [from_above, jnp.zeros((LAT_DEV - SIDE, LON_DEV, D), jnp.bfloat16), from_below], axis=0
    )
    return main[MARGIN:-MARGIN] + extra.astype(jnp.float32)


STAGES = (2, 4, 4, 4)
LEFT = (512, 128, 32, 8)


def place():
    lon = lax.axis_index("lon")
    return lax.axis_index("dp"), lax.axis_index("lat"), lon >> 3, (lon >> 1) & 3, lon & 1


def device(xlo, y, xhi, z, core):
    return (xlo, y, xhi * 8 + z * 2 + core)


def peers(stage):
    xlo, y, xhi, z, core = place()
    if stage == 0:
        return core, [(1 - core, device(xlo, y, xhi, z, 1 - core))]
    me = (None, z, y, xhi * 2 + xlo)[stage]
    others = []
    for step in (1, 3, 2):
        to = (me + step) & 3
        if stage == 1:
            others.append((to, device(xlo, y, xhi, to, core)))
        elif stage == 2:
            others.append((to, device(xlo, to, xhi, z, core)))
        else:
            others.append((to, device(to & 1, y, to >> 1, z, core)))
    return me, others


def reduce_kernel(quads, part, out, held1, held2, held3, got0, got1, got2, got3, send, recv):
    held = (part, held1, held2, held3)
    got = (got0, got1, got2, got3)
    barrier = pltpu.get_barrier_semaphore()
    count = 0
    for stage in range(4):
        for _, dev in peers(stage)[1]:
            pl.semaphore_signal(barrier, inc=1, device_id=dev, device_id_type=MESH)
            count += 1
    pl.semaphore_wait(barrier, count)

    def copies(c, stage):
        _, others = peers(stage)
        return [
            pltpu.make_async_remote_copy(
                src_ref=held[stage].at[c, :, pl.ds(to * LEFT[stage], LEFT[stage]), :],
                dst_ref=got[stage].at[c, n],
                send_sem=send.at[c, stage, n],
                recv_sem=recv.at[c, stage, n],
                device_id=dev,
                device_id_type=MESH,
            )
            for n, (to, dev) in enumerate(others)
        ]

    def finish(c, stage):
        for copy in copies(c, stage):
            copy.wait()
        me, others = peers(stage)
        rows = pl.ds(pl.multiple_of(me * LEFT[stage], LEFT[stage]), LEFT[stage])
        value = held[stage][c, :, rows, :].astype(jnp.float32)
        for n in range(len(others)):
            value = value + got[stage][c, n].astype(jnp.float32)
        if stage == 3:
            out[c] = value
        else:
            held[stage + 1][c] = value.astype(held[stage + 1].dtype)

    for tick in range(quads + 4):
        for stage in range(4, -1, -1):
            c = tick - stage
            if 0 <= c < quads:
                if stage > 0:
                    finish(c, stage - 1)
                if stage < 4:
                    for copy in copies(c, stage):
                        copy.start()


def reduced(part):
    quads = part.shape[0]
    kinds = (jnp.bfloat16, jnp.bfloat16, jnp.bfloat16, jnp.float32)
    held = [pltpu.VMEM((quads, 3, LEFT[s - 1], WIDTH), kinds[s]) for s in range(1, 4)]
    got = [pltpu.VMEM((quads, STAGES[s] - 1, 3, LEFT[s], WIDTH), kinds[s]) for s in range(4)]
    sems = [pltpu.SemaphoreType.DMA((quads, 4, 3)), pltpu.SemaphoreType.DMA((quads, 4, 3))]
    return pl.pallas_call(
        functools.partial(reduce_kernel, quads),
        out_shape=jax.ShapeDtypeStruct((quads, 3, 8, WIDTH), jnp.float32),
        in_specs=[pl.BlockSpec(memory_space=pltpu.VMEM)],
        out_specs=pl.BlockSpec(memory_space=pltpu.VMEM),
        scratch_shapes=held + got + sems,
        compiler_params=pltpu.CompilerParams(
            collective_id=0, has_side_effects=True, vmem_limit_bytes=40 * 2**20
        ),
        name="reduce_weights",
    )(part)


def body(inputs, grad_out, w_qkv):
    scale = float(2 * 128 * 256) ** -0.5
    x = extended(inputs)
    gw, gi = attention(x, grad_out.reshape(OWN_N, D), w_qkv, scale)
    grad_inputs = given_back(gi).astype(jnp.bfloat16)[None]
    out = reduced(gw)
    grad_w = out.transpose(2, 1, 0, 3).reshape(8, 3 * D)
    return grad_inputs, grad_w


def solution(mesh):
    in_specs = (P("dp", "lat", "lon", None), P("dp", "lat", "lon", None), P())
    out_specs = (P("dp", "lat", "lon", None), P(("dp", "lat", "lon"), None))
    return jax.shard_map(body, mesh=mesh, in_specs=in_specs, out_specs=out_specs, check_vma=False)
```

time: 1250 us -> 189 us (0.15); the launches traced: 1230 us -> 189 us
  waiting for transfers between devices: 727 us -> 27.5 us
  local copies, waits for them, and re-layouts: 287 us -> 11.4 us
  Pallas kernels: 0 us -> 120 us
  other arithmetic: 109 us -> 7.64 us
  matrix products: 71.7 us -> 0 us
  between operations: 22.1 us -> 0.8 us
    unnamed x2 -> x0, waiting for transfers between devices: 648 us -> none
    pallas_call x0 -> x2, Pallas kernels: none -> 120 us  [the longest x1 60.9 us: attention(): pl.pallas_call(functools.partial(attention_kernel, scale, unroll), grid=(...]
    dynamic_update_slice x4 -> x0, local copies, waits for them, and re-layouts: 81.3 us -> none  [group_step(): lax.dynamic_update_slice(totals, current + region_grads[member].reshape(1...]
    dot_general x7 -> x0, matrix products: 59.1 us -> none  [the longest x1 14.2 us: tile_grads(): jnp.einsum('khd,ihd->hki', head_values, head_grads, preferred_element_typ...]
    ppermute x8, waiting for transfers between devices: 79.9 us -> 27.5 us  [shifted(): return lax.ppermute(block, axis, route)]
    slice x16 -> x8, local copies, waits for them, and re-layouts: 54.2 us -> 4.05 us  [the longest x1 1.77 us: given_back(): gi[SPLIT:SPLIT + (LAT_DEV + SIDE) * SIDE].reshape(LAT_DEV + SIDE, SIDE, D)]
    concatenate x4 -> x3, other arithmetic: 51.1 us -> 4.1 us  [the longest x1 3.18 us: extended(): return jnp.concatenate([lead, tall.reshape(-1, D), sides, end], axis=0)]
    reshape x6 -> x2, local copies, waits for them, and re-layouts: 40.4 us -> 2.02 us  [the longest x1 1.32 us: extended(): sides = jnp.concatenate([left, right], axis=1).reshape(-1, D)]
  transfers between devices with their start and end apart: 9 -> 8, of which waited for: 5 -> 5; matrix products, arithmetic and copies ran while one was open for 5% -> 1% of each run, Pallas kernels for 0% -> 31%
where the time goes in v1:
time: 189 us
  Pallas kernels  120 us (63%)
  waiting for transfers between devices  27.5 us (15%)
  starting transfers between devices  21.2 us (11%)
  local copies, waits for them, and re-layouts  11.4 us (6%)
  other arithmetic  7.64 us (4%)
    pallas_call x1, Pallas kernels, attention(): pl.pallas_call(functools.partial(attention_kernel, scale, unroll), grid=(...  60.9 us
    pallas_call x1, Pallas kernels, reduced(): pl.pallas_call(functools.partial(reduce_kernel, quads), out_shape=jax.Sha...  59.1 us
    ppermute x8, waiting for transfers between devices, shifted(): return lax.ppermute(block, axis, route)  27.5 us
    ppermute x8, starting transfers between devices, shifted(): return lax.ppermute(block, axis, route)  21.2 us
  transfers between devices with their start and end apart: 8, of which 5 were waited for; matrix products, arithmetic and copies ran while one was open for 1% of the time, Pallas kernels for 31%

profile of v1, /device:TPU:0, one launch (start us, length us, event | category | flops | bytes accessed | tf_op | source)
XLA Modules:
  0.0 188.6 jit_solution(12951024832541072013)
XLA Ops:
  0.6 1.8 copy.20
  2.5 3.6 %collective-permute-start = (bf16[6,16,1024]{2,0,1:T(8,128)(2,1)S(1)}, bf16[6,16,1024]{2,0,1:T(8,128)(2,1)S(1)}, u32[]{:S(2)}, u32[]{:S(2)}) collective-permute-start(bf16[6,16,1024]{2,0,1:T(8,128)(2,1)S(1)} %get-tuple-element.16), channel_id=1, source_target_pairs={{0,16},{16,32},{32,48},{1,17},{17,33},{33,49},{2,18},{18,34},{34,5... | collective-permute-start | bytes 589832 | tf_op jit(solution)/shard_map/ppermute | solution.py:221
  6.1 1.3 collective-permute-start.1
  7.4 4.2 %collective-permute-done = bf16[6,16,1024]{2,0,1:T(8,128)(2,1)S(1)} collective-permute-done((bf16[6,16,1024]{2,0,1:T(8,128)(2,1)S(1)}, bf16[6,16,1024]{2,0,1:T(8,128)(2,1)S(1)}, u32[]{:S(2)}, u32[]{:S(2)}) %collective-permute-start) | collective-permute-done | bytes 196640 | tf_op jit(solution)/shard_map/ppermute | solution.py:221
  11.6 4.1 %collective-permute-done.1 = bf16[6,16,1024]{2,0,1:T(8,128)(2,1)S(1)} collective-permute-done((bf16[6,16,1024]{2,0,1:T(8,128)(2,1)S(1)}, bf16[6,16,1024]{2,0,1:T(8,128)(2,1)S(1)}, u32[]{:S(2)}, u32[]{:S(2)}) %collective-permute-start.1) | collective-permute-done | bytes 196640 | tf_op jit(solution)/shard_map/ppermute | solution.py:221
  15.8 0.8 pad_maximum_fusion
  16.6 0.1 fusion.4
  16.7 5.3 %collective-permute-start.3 = (bf16[44,6,1024]{2,0,1:T(8,128)(2,1)S(1)}, bf16[44,6,1024]{2,0,1:T(8,128)(2,1)S(1)}, u32[]{:S(2)}, u32[]{:S(2)}) collective-permute-start(bf16[44,6,1024]{2,0,1:T(8,128)(2,1)S(1)} %get-tuple-element.13), channel_id=1, source_target_pairs={{0,15},{1,0},{2,1},{3,2},{4,3},{5,4},{6,5},{7,6},{8,7},{9,8},{10,9... | collective-permute-start | bytes 1622024 | tf_op jit(solution)/shard_map/ppermute | solution.py:221
  22.2 0.8 copy.9
  23.0 6.7 %collective-permute-done.2 = bf16[44,6,1024]{2,0,1:T(8,128)(2,1)S(1)} collective-permute-done((bf16[44,6,1024]{2,0,1:T(8,128)(2,1)S(1)}, bf16[44,6,1024]{2,0,1:T(8,128)(2,1)S(1)}, u32[]{:S(2)}, u32[]{:S(2)}) %collective-permute-start.2) | collective-permute-done | bytes 540704 | tf_op jit(solution)/shard_map/ppermute | solution.py:221
  29.7 0.1 pad_maximum_fusion.1
  29.8 0.6 copy.10
  30.4 1.3 reshape.24
  31.7 3.2 %maximum_maximum_fusion.x = bf16[1280,1024]{1,0:T(8,128)(2,1)} fusion(bf16[528,1024]{1,0:T(8,128)(2,1)} %reshape.24, bf16[704,1024]{1,0:T(8,128)(2,1)S(1)} %bitcast.18, bf16[1280]{0:T(1024)(128)(2,1)S(1)} %pad.9.clone, bf16[1280]{0:T(1024)(128)(2,1)S(1)} %pad.6.clone), kind=kLoop, calls=%fused_computation.1 | loop fusion | flops 10485760 | bytes 5149696 | tf_op jit(solution)/shard_map/concatenate | solution.py:234
  34.9 60.9 %attention.1 = (bf16[4,3,1024,256]{3,2,1,0:T(8,128)(2,1)}, f32[1280,1024]{1,0:T(8,128)}) custom-call(bf16[1280,1024]{1,0:T(8,128)(2,1)} %maximum_maximum_fusion.x, bf16[512,1024]{1,0:T(8,128)(2,1)} %bitcast.19, bf16[1024,3072]{1,0:T(8,128)(2,1)} %wv.1, bf16[1024,3072]{1,0:T(8,128)(2,1)} %wv.1, bf16[1024,3072]{1,0:T(8,128)(2,1)} %wv.1), custom_call_target="tpu_custom_call" | custom-call | tf_op jit(solution)/shard_map/attention/pallas_call | solution.py:194
  95.8 1.8 slice.73
  97.6 0.3 convert_element_type.15
  97.9 0.4 fusion.5
  98.3 0.3 copy.11
  98.6 0.3 copy.12
  98.9 5.4 %collective-permute-start.5 = (bf16[44,6,1024]{2,0,1:T(8,128)(2,1)S(1)}, bf16[44,6,1024]{2,0,1:T(8,128)(2,1)S(1)}, u32[]{:S(2)}, u32[]{:S(2)}) collective-permute-start(bf16[44,6,1024]{2,0,1:T(8,128)(2,1)S(1)} %copy.12), channel_id=1, source_target_pairs={{0,15},{1,0},{2,1},{3,2},{4,3},{5,4},{6,5},{7,6},{8,7},{9,8},{10,9... | collective-permute-start | bytes 1622024 | tf_op jit(solution)/shard_map/ppermute | solution.py:221
  104.4 0.3 slice.48
  104.8 7.0 %collective-permute-done.5 = bf16[44,6,1024]{2,0,1:T(8,128)(2,1)S(1)} collective-permute-done((bf16[44,6,1024]{2,0,1:T(8,128)(2,1)S(1)}, bf16[44,6,1024]{2,0,1:T(8,128)(2,1)S(1)}, u32[]{:S(2)}, u32[]{:S(2)}) %collective-permute-start.5) | collective-permute-done | bytes 540704 | tf_op jit(solution)/shard_map/ppermute | solution.py:221
  111.7 5.5 %collective-permute-done.4 = bf16[44,6,1024]{2,0,1:T(8,128)(2,1)S(1)} collective-permute-done((bf16[44,6,1024]{2,0,1:T(8,128)(2,1)S(1)}, bf16[44,6,1024]{2,0,1:T(8,128)(2,1)S(1)}, u32[]{:S(2)}, u32[]{:S(2)}) %collective-permute-start.4) | collective-permute-done | bytes 540704 | tf_op jit(solution)/shard_map/ppermute | solution.py:221
  117.3 2.0 %fusion.2 = (bf16[44,16,1024]{2,0,1:T(8,128)(2,1)S(1)}, f32[44,16,1024]{2,0,1:T(8,128)S(1)}) fusion(bf16[44,6,1024]{2,0,1:T(8,128)(2,1)S(1)} %collective-permute-done.5, bf16[16]{0:T(256)(128)(2,1)S(1)} %pad.4.clone, bf16[44,6,1024]{2,0,1:T(8,128)(2,1)S(1)} %collective-permute-done.4, f32[44,16,1024]{2,1,0:T(8,128)S(1)} %bitcast.16), kind=kLoop, calls=%fused_computation.11 | loop fusion | flops 3604480 | bytes 8290336 | tf_op jit(solution)/shard_map/convert.1
  119.2 0.8 fusion.3
  120.1 4.2 %collective-permute-start.6 = (bf16[6,16,1024]{2,0,1:T(8,128)(2,1)}, bf16[6,16,1024]{2,0,1:T(8,128)(2,1)}, u32[]{:S(2)}, u32[]{:S(2)}) collective-permute-start(bf16[6,16,1024]{2,0,1:T(8,128)(2,1)} %get-tuple-element.10), channel_id=1, source_target_pairs={{0,16},{16,32},{32,48},{1,17},{17,33},{33,49},{2,18},{18,34},{34,5... | collective-permute-start | bytes 589832 | tf_op jit(solution)/shard_map/ppermute | solution.py:221
  124.2 1.3 collective-permute-start.7
  125.6 59.1 %reduce_weights.1 = f32[4,3,8,256]{3,2,1,0:T(8,128)S(1)} custom-call(bf16[4,3,1024,256]{3,2,1,0:T(8,128)(2,1)S(1)} %bitcast.14), custom_call_target="tpu_custom_call" | custom-call | tf_op jit(solution)/shard_map/reduce_weights/pallas_call | solution.py:340
  184.8 0.7 reshape.27
  185.5 1.5 fusion.1
  187.1 1.5 copy.15
  (22 shorter events, 0.5 us)
Async XLA Ops:
  2.5 9.1 %collective-permute-start = (bf16[6,16,1024]{2,0,1:T(8,128)(2,1)S(1)}, bf16[6,16,1024]{2,0,1:T(8,128)(2,1)S(1)}, u32[]{:S(2)}, u32[]{:S(2)}) collective-permute-start(bf16[6,16,1024]{2,0,1:T(8,128)(2,1)S(1)} %get-tuple-element.16), channel_id=1, source_target_pairs={{0,16},{16,32},{32,48},{1,17},{17,33},{33,49},{2,18},{18,34},{34,5... | collective-permute-start | bytes 589832 | tf_op jit(solution)/shard_map/ppermute | solution.py:221
  6.1 9.7 %collective-permute-start.1 = (bf16[6,16,1024]{2,0,1:T(8,128)(2,1)S(1)}, bf16[6,16,1024]{2,0,1:T(8,128)(2,1)S(1)}, u32[]{:S(2)}, u32[]{:S(2)}) collective-permute-start(bf16[6,16,1024]{2,0,1:T(8,128)(2,1)S(1)} %get-tuple-element.17), channel_id=1, source_target_pairs={{16,0},{32,16},{48,32},{17,1},{33,17},{49,33},{18,2},{34,18},{50,3... | collective-permute-start | bytes 589832 | tf_op jit(solution)/shard_map/ppermute | solution.py:221
  16.7 13.0 %collective-permute-start.2 = (bf16[44,6,1024]{2,0,1:T(8,128)(2,1)S(1)}, bf16[44,6,1024]{2,0,1:T(8,128)(2,1)S(1)}, u32[]{:S(2)}, u32[]{:S(2)}) collective-permute-start(bf16[44,6,1024]{2,0,1:T(8,128)(2,1)S(1)} %get-tuple-element.12), channel_id=1, source_target_pairs={{0,1},{1,2},{2,3},{3,4},{4,5},{5,6},{6,7},{7,8},{8,9},{9,10},{10,1... | collective-permute-start | bytes 1622024 | tf_op jit(solution)/shard_map/ppermute | solution.py:221
  16.7 12.9 %collective-permute-start.3 = (bf16[44,6,1024]{2,0,1:T(8,128)(2,1)S(1)}, bf16[44,6,1024]{2,0,1:T(8,128)(2,1)S(1)}, u32[]{:S(2)}, u32[]{:S(2)}) collective-permute-start(bf16[44,6,1024]{2,0,1:T(8,128)(2,1)S(1)} %get-tuple-element.13), channel_id=1, source_target_pairs={{0,15},{1,0},{2,1},{3,2},{4,3},{5,4},{6,5},{7,6},{8,7},{9,8},{10,9... | collective-permute-start | bytes 1622024 | tf_op jit(solution)/shard_map/ppermute | solution.py:221
  97.9 6.5 %copy-start = (f32[1280,1024]{1,0:T(8,128)S(1)}, f32[1280,1024]{1,0:T(8,128)}, u32[]{:S(2)}) copy-start(f32[1280,1024]{1,0:T(8,128)} %get-tuple-element.4) | copy-start | bytes 15728644
  98.9 12.8 %collective-permute-start.5 = (bf16[44,6,1024]{2,0,1:T(8,128)(2,1)S(1)}, bf16[44,6,1024]{2,0,1:T(8,128)(2,1)S(1)}, u32[]{:S(2)}, u32[]{:S(2)}) collective-permute-start(bf16[44,6,1024]{2,0,1:T(8,128)(2,1)S(1)} %copy.12), channel_id=1, source_target_pairs={{0,15},{1,0},{2,1},{3,2},{4,3},{5,4},{6,5},{7,6},{8,7},{9,8},{10,9... | collective-permute-start | bytes 1622024 | tf_op jit(solution)/shard_map/ppermute | solution.py:221
  104.3 12.9 %collective-permute-start.4 = (bf16[44,6,1024]{2,0,1:T(8,128)(2,1)S(1)}, bf16[44,6,1024]{2,0,1:T(8,128)(2,1)S(1)}, u32[]{:S(2)}, u32[]{:S(2)}) collective-permute-start(bf16[44,6,1024]{2,0,1:T(8,128)(2,1)S(1)} %copy.11), channel_id=1, source_target_pairs={{0,1},{1,2},{2,3},{3,4},{4,5},{5,6},{6,7},{7,8},{8,9},{9,10},{10,1... | collective-permute-start | bytes 1622024 | tf_op jit(solution)/shard_map/ppermute | solution.py:221
  104.4 21.2 %slice-start = ((s8[6291456]{0:T(1024)(128)(4,1)}), s8[4194304]{0:T(1024)(128)(4,1)S(1)}, s32[]{:S(2)}) async-start(s8[6291456]{0:T(1024)(128)(4,1)} %bitcast.13), calls=%async_computation | async-start | bytes 8388608
  117.3 8.4 %slice-start.1 = ((s8[6291456]{0:T(1024)(128)(4,1)}), s8[2097152]{0:T(1024)(128)(4,1)S(1)}, s32[]{:S(2)}) async-start(s8[6291456]{0:T(1024)(128)(4,1)} %bitcast.13), calls=%async_computation.1 | async-start | bytes 4194304
  120.1 65.4 %collective-permute-start.6 = (bf16[6,16,1024]{2,0,1:T(8,128)(2,1)}, bf16[6,16,1024]{2,0,1:T(8,128)(2,1)}, u32[]{:S(2)}, u32[]{:S(2)}) collective-permute-start(bf16[6,16,1024]{2,0,1:T(8,128)(2,1)} %get-tuple-element.10), channel_id=1, source_target_pairs={{0,16},{16,32},{32,48},{1,17},{17,33},{33,49},{2,18},{18,34},{34,5... | collective-permute-start | bytes 589832 | tf_op jit(solution)/shard_map/ppermute | solution.py:221
  124.2 61.3 %collective-permute-start.7 = (bf16[6,16,1024]{2,0,1:T(8,128)(2,1)S(1)}, bf16[6,16,1024]{2,0,1:T(8,128)(2,1)}, u32[]{:S(2)}, u32[]{:S(2)}) collective-permute-start(bf16[6,16,1024]{2,0,1:T(8,128)(2,1)S(1)} %get-tuple-element.11), channel_id=1, source_target_pairs={{16,0},{32,16},{48,32},{17,1},{33,17},{49,33},{18,2},{34,18},{50,3... | collective-permute-start | bytes 589832 | tf_op jit(solution)/shard_map/ppermute | solution.py:221

commit v2 on v1

v2 whole, which is shorter than its diff:
```python
import functools

import jax
import jax.numpy as jnp
import numpy as np
from jax import lax
from jax.experimental import pallas as pl
from jax.experimental.pallas import tpu as pltpu
from jax.sharding import PartitionSpec as P

WIN = 13
MARGIN = WIN // 2
HEAD = 64
QUAD = 4
WIDTH = QUAD * HEAD
LAT_DEV = 32
LON_DEV = 16
ROW_T = 4
TILES = LAT_DEV // ROW_T
QUERIES = ROW_T * LON_DEV
KEY_ROWS = ROW_T + WIN - 1
SIDE = 2 * MARGIN
KEYS_A = KEY_ROWS * LON_DEV
KEYS_B = KEY_ROWS * SIDE
KEYS = KEYS_A + KEYS_B
PAD_ROWS = 2
OWN = (PAD_ROWS + MARGIN) * LON_DEV
OWN_N = LAT_DEV * LON_DEV
SPLIT = (PAD_ROWS + LAT_DEV + SIDE) * LON_DEV
TOKENS = 1280
D = 1024
NT = (((1,), (1,)), ((), ()))
TN = (((0,), (0,)), ((), ()))
NN = (((1,), (0,)), ((), ()))
MESH = pl.DeviceIdType.MESH


def mm(a, b, dims=NN):
    return lax.dot_general(a, b, dims, preferred_element_type=jnp.float32)


def key_tile(t, first_band, last_band):
    lead = jnp.logical_and(first_band, t == 0).astype(jnp.int32)
    tail = jnp.logical_and(last_band, t == TILES - 1).astype(jnp.int32)
    return t + lead - tail


def window_bias(t, top, keys, side, band_start, total_rows):
    kk = lax.broadcasted_iota(jnp.int32, (keys, WIDTH), 0)
    qq = lax.broadcasted_iota(jnp.int32, (keys, WIDTH), 1) & (QUERIES - 1)
    i, j = qq >> 4, qq & 15
    if side:
        r = (kk * 171) >> 11
        c = kk - r * SIDE
        col = jnp.where(c < MARGIN, c - MARGIN, c + (LON_DEV - MARGIN))
    else:
        r, col = kk >> 4, kk & 15
    first = band_start + ROW_T * t
    key_row = band_start + ROW_T * top - MARGIN + r
    start = jnp.clip(first + i - MARGIN, 0, total_rows - WIN)
    off = key_row - start
    away = col - j
    inside = (off >= 0) & (off < WIN) & (away >= -MARGIN) & (away <= MARGIN)
    return jnp.where(inside, 0.0, -1e30).astype(jnp.float32)


def spread(tile, same_head):
    return jnp.concatenate([tile] * QUAD, axis=0) * same_head


def attend(t, top, cols, q, kv, vv, go, bias, same, dk, dv, dq):
    own = pl.ds(t * QUERIES, QUERIES)
    ka = pl.ds(pl.multiple_of(PAD_ROWS * LON_DEV + top * QUERIES, 32), KEYS_A)
    kb = pl.ds(pl.multiple_of(SPLIT + top * ROW_T * SIDE, 16), KEYS_B)
    same_head = same[...]
    bq = spread(q[own, cols], same_head)
    bg = spread(go[own, cols], same_head)
    keys_a, keys_b = kv[ka, cols], kv[kb, cols]
    sa = mm(keys_a, bq, NT) + bias[t, :KEYS_A, :]
    sb = mm(keys_b, bq, NT) + bias[t, KEYS_A:, :]
    peak = jnp.maximum(jnp.max(sa, axis=0, keepdims=True), jnp.max(sb, axis=0, keepdims=True))
    pa = jnp.exp(sa - peak)
    pb = jnp.exp(sb - peak)
    da = mm(vv[ka, cols], bg, NT)
    db = mm(vv[kb, cols], bg, NT)
    inv = 1.0 / (jnp.sum(pa, axis=0, keepdims=True) + jnp.sum(pb, axis=0, keepdims=True))
    delta = (
        jnp.sum(pa * da, axis=0, keepdims=True) + jnp.sum(pb * db, axis=0, keepdims=True)
    ) * inv
    pa = pa * inv
    pb = pb * inv
    aa = pa.astype(jnp.bfloat16)
    ab = pb.astype(jnp.bfloat16)
    ea = (pa * (da - delta)).astype(jnp.bfloat16)
    eb = (pb * (db - delta)).astype(jnp.bfloat16)
    dk[ka, :] += mm(ea, bq)
    dk[kb, :] += mm(eb, bq)
    dv[ka, :] += mm(aa, bg)
    dv[kb, :] += mm(ab, bg)
    mixed = (mm(ea, keys_a, TN) + mm(eb, keys_b, TN)) * same_head.astype(jnp.float32)
    total = mixed[:QUERIES]
    for h in range(1, QUAD):
        total = total + mixed[h * QUERIES : (h + 1) * QUERIES]
    rows = pl.ds(OWN + t * QUERIES, QUERIES)
    dq[rows, cols] = (total * HEAD**-0.5).astype(jnp.bfloat16)


def feature_order(block):
    row = lax.broadcasted_iota(jnp.int32, (256, D), 0) + block * 256
    col = lax.broadcasted_iota(jnp.int32, (256, D), 1)
    r = row & 7
    xlo = (row >> 3) & 1
    xhi = (row >> 4) & 1
    y = (row >> 5) & 3
    z = (row >> 7) & 3
    core = row >> 9
    source = (((((xlo * 4 + y) * 2 + xhi) * 4 + z) * 2 + core) << 3) + r
    return jnp.where(col == source, 1.0, 0.0).astype(jnp.bfloat16)


STAGES = (2, 4, 4, 4)
LEFT = (512, 128, 32, 8)


def place():
    lon = lax.axis_index("lon")
    return lax.axis_index("dp"), lax.axis_index("lat"), lon >> 3, (lon >> 1) & 3, lon & 1


def device(xlo, y, xhi, z, core):
    return (xlo, y, xhi * 8 + z * 2 + core)


def peers(stage):
    xlo, y, xhi, z, core = place()
    if stage == 0:
        return core, [(1 - core, device(xlo, y, xhi, z, 1 - core))]
    me = (None, z, y, xhi * 2 + xlo)[stage]
    others = []
    for step in (1, 3, 2):
        to = (me + step) & 3
        if stage == 1:
            others.append((to, device(xlo, y, xhi, to, core)))
        elif stage == 2:
            others.append((to, device(xlo, to, xhi, z, core)))
        else:
            others.append((to, device(to & 1, y, to >> 1, z, core)))
    return me, others


SLOTS = ((0, 192, 0, -1), (192, 192, 0, 1), (384, 48, -1, -1), (432, 48, -1, 1), (480, 48, 1, -1), (528, 48, 1, 1))
OPPOSITE = (1, 0, 5, 4, 3, 2)
PACKED = 576
SIDES = TOKENS - SPLIT
ABOVE = PAD_ROWS * LON_DEV
BELOW = OWN + OWN_N
BAND = MARGIN * LON_DEV
QUADS = D // WIDTH


def packing():
    pack = np.zeros((PACKED, OWN_N), np.float32)
    side = np.zeros((SIDES, PACKED), np.float32)
    for start, size, dy, dx in SLOTS:
        count = LAT_DEV if dy == 0 else MARGIN
        for r in range(count):
            for c in range(MARGIN):
                row = r + (LAT_DEV - MARGIN if dy > 0 else 0)
                col = c + (LON_DEV - MARGIN if dx > 0 else 0)
                pack[start + r * MARGIN + c, row * LON_DEV + col] = 1
                row = r + (MARGIN if dy == 0 else 0 if dy < 0 else LAT_DEV + MARGIN)
                col = c + (MARGIN if dx > 0 else 0)
                side[row * SIDE + col, start + r * MARGIN + c] = 1
    return jnp.asarray(pack, jnp.bfloat16), jnp.asarray(side, jnp.bfloat16)


def fused_kernel(
    scale, x, pack, go_hbm, w_hbm, side_hbm, gi, gw,
    go, w, side, xe, packed, halo, q, k, v, dall, dk, dv, bias, same, xt,
    part, held1, held2, held3, got0, got1, got2, got3,
    edge, back, lat_out, lat_in, own_grad,
    load, send, recv, halo_send, halo_recv, back_send, back_recv,
):
    dp, lat, lon = lax.axis_index("dp"), lax.axis_index("lat"), lax.axis_index("lon")
    lats, lons = lax.axis_size("lat"), lax.axis_size("lon")
    band_start = lat * LAT_DEV
    total_rows = LAT_DEV * lats
    first_band, last_band = lat == 0, lat == lats - 1
    held = (part, held1, held2, held3)
    got = (got0, got1, got2, got3)

    loads = [
        pltpu.make_async_copy(w_hbm, w, load.at[0]),
        pltpu.make_async_copy(go_hbm, go, load.at[1]),
        pltpu.make_async_copy(side_hbm, side, load.at[2]),
    ]
    for copy in loads:
        copy.start()

    def when_there(dy, act):
        if dy == 0:
            act()
        else:
            pl.when(lat > 0 if dy < 0 else lat < lats - 1)(act)

    def neighbour(dy, dx):
        return (dp, lat + dy, lax.rem(lon + dx + lons, lons))

    moves = [(dy, dx) for _, _, dy, dx in SLOTS] + [(-1, 0), (1, 0)]

    packed[...] = mm(pack[...], x[...]).astype(jnp.bfloat16)

    barrier = pltpu.get_barrier_semaphore()
    count = 0
    for stage in range(4):
        for _, dev in peers(stage)[1]:
            pl.semaphore_signal(barrier, inc=1, device_id=dev, device_id_type=MESH)
            count += 1
    for dy, dx in moves:
        @functools.partial(when_there, dy)
        def _():
            pl.semaphore_signal(barrier, inc=1, device_id=neighbour(dy, dx), device_id_type=MESH)
    count = count + 2 + 3 * (lat > 0).astype(jnp.int32) + 3 * (lat < lats - 1).astype(jnp.int32)
    pl.semaphore_wait(barrier, count)

    def exchange(source, target, up, down, into_up, into_down, sends, recvs, sending):
        for n, (dy, dx) in enumerate(moves):
            @functools.partial(when_there, dy)
            def _():
                if n < 6:
                    other = OPPOSITE[n]
                    start, size = SLOTS[n][:2]
                    there = SLOTS[other][0]
                    src = source.at[pl.ds(start, size), :]
                    far, near = target.at[pl.ds(there, size), :], target.at[pl.ds(start, size), :]
                else:
                    other = 13 - n
                    src = (up, down)[n - 6]
                    far, near = (into_down, into_up) if n == 6 else (into_up, into_down)
                copy = pltpu.make_async_remote_copy(
                    src_ref=src,
                    dst_ref=far if sending else near,
                    send_sem=sends.at[n],
                    recv_sem=recvs.at[other if sending else n],
                    device_id=neighbour(dy, dx),
                    device_id_type=MESH,
                )
                if sending:
                    copy.start()
                else:
                    copy.wait()

    def halo_exchange(sending):
        exchange(
            packed, halo, x.at[pl.ds(0, BAND), :], x.at[pl.ds(OWN_N - BAND, BAND), :],
            xe.at[pl.ds(ABOVE, BAND), :], xe.at[pl.ds(BELOW, BAND), :],
            halo_send, halo_recv, sending,
        )

    def give_back(sending):
        exchange(
            edge, back, lat_out.at[pl.ds(0, BAND), :], lat_out.at[pl.ds(BAND, BAND), :],
            lat_in.at[pl.ds(0, BAND), :], lat_in.at[pl.ds(BAND, BAND), :],
            back_send, back_recv, sending,
        )

    halo_exchange(True)

    for there, slot in ((lat > 0, 384), (lat < lats - 1, 480)):
        @pl.when(jnp.logical_not(there))
        def _():
            zero = jnp.zeros((96, D), jnp.bfloat16)
            halo[slot : slot + 96, :] = zero
            back[slot : slot + 96, :] = zero
            at = ABOVE if slot == 384 else BELOW
            xe[at : at + BAND, :] = zero
            at = 0 if slot == 384 else BAND
            lat_in[at : at + BAND, :] = zero

    xe[:ABOVE, :] = jnp.zeros((ABOVE, D), jnp.bfloat16)
    xe[OWN : OWN + OWN_N, :] = x[...]
    row = lax.broadcasted_iota(jnp.int32, (WIDTH, WIDTH), 0)
    col = lax.broadcasted_iota(jnp.int32, (WIDTH, WIDTH), 1)
    same[...] = jnp.where((row >> 6) == (col >> 6), 1.0, 0.0).astype(jnp.bfloat16)

    loads[0].wait()

    @pl.loop(0, QUADS)
    def _(b):
        cols = pl.ds(pl.multiple_of(b * WIDTH, WIDTH), WIDTH)
        kcols = pl.ds(pl.multiple_of(D + b * WIDTH, WIDTH), WIDTH)
        vcols = pl.ds(pl.multiple_of(2 * D + b * WIDTH, WIDTH), WIDTH)
        q[:, cols] = mm(x[...], w[:, cols]).astype(jnp.bfloat16) * jnp.bfloat16(0.125)
        k[OWN : OWN + OWN_N, cols] = mm(x[...], w[:, kcols]).astype(jnp.bfloat16)
        v[OWN : OWN + OWN_N, cols] = mm(x[...], w[:, vcols]).astype(jnp.bfloat16)

    @pl.loop(0, TILES)
    def _(t):
        top = key_tile(t, first_band, last_band)
        bias[t, :KEYS_A, :] = window_bias(t, top, KEYS_A, False, band_start, total_rows)
        bias[t, KEYS_A:, :] = window_bias(t, top, KEYS_B, True, band_start, total_rows)

    loads[1].wait()
    loads[2].wait()
    halo_exchange(False)
    xe[SPLIT:, :] = mm(side[...], halo[...]).astype(jnp.bfloat16)

    @pl.loop(0, QUADS)
    def _(b):
        cols = pl.ds(pl.multiple_of(b * WIDTH, WIDTH), WIDTH)
        kcols = pl.ds(pl.multiple_of(D + b * WIDTH, WIDTH), WIDTH)
        vcols = pl.ds(pl.multiple_of(2 * D + b * WIDTH, WIDTH), WIDTH)
        outer = jnp.concatenate([xe[:OWN, :], xe[BELOW:, :]], axis=0)
        for into, wcols in ((k, kcols), (v, vcols)):
            value = mm(outer, w[:, wcols]).astype(jnp.bfloat16)
            into[:OWN, cols] = value[:OWN]
            into[BELOW:, cols] = value[OWN:]
        rows = pl.ds(pl.multiple_of(b * 256, 256), 256)
        xt[rows, :] = mm(feature_order(b), xe[...], NT).astype(jnp.bfloat16)

    def copies(c, stage):
        return [
            pltpu.make_async_remote_copy(
                src_ref=held[stage].at[c, :, pl.ds(to * LEFT[stage], LEFT[stage]), :],
                dst_ref=got[stage].at[c, n],
                send_sem=send.at[c, stage, n],
                recv_sem=recv.at[c, stage, n],
                device_id=dev,
                device_id_type=MESH,
            )
            for n, (to, dev) in enumerate(peers(stage)[1])
        ]

    def begin(c, stage):
        for copy in copies(c, stage):
            copy.start()

    def finish(c, stage):
        for copy in copies(c, stage):
            copy.wait()
        me, others = peers(stage)
        rows = pl.ds(pl.multiple_of(me * LEFT[stage], LEFT[stage]), LEFT[stage])
        for i in range(3):
            value = held[stage][c, i, rows, :].astype(jnp.float32)
            for n in range(len(others)):
                value = value + got[stage][c, n, i].astype(jnp.float32)
            if stage == 3:
                at = i * D + c * WIDTH
                gw[:, pl.ds(at if isinstance(at, int) else pl.multiple_of(at, WIDTH), WIDTH)] = value
            else:
                held[stage + 1][c, i] = value.astype(held[stage + 1].dtype)
        if stage < 3:
            begin(c, stage + 1)

    @pl.loop(0, QUADS)
    def _(g):
        cols = pl.ds(pl.multiple_of(g * WIDTH, WIDTH), WIDTH)
        kcols = pl.ds(pl.multiple_of(D + g * WIDTH, WIDTH), WIDTH)
        vcols = pl.ds(pl.multiple_of(2 * D + g * WIDTH, WIDTH), WIDTH)
        dk[...] = jnp.zeros_like(dk)
        dv[...] = jnp.zeros_like(dv)

        def tiles(a, b):
            for t in range(a, b):
                top = key_tile(t, first_band, last_band)
                attend(t, top, cols, q, k, v, go, bias, same, dk, dv, dall)

        tiles(0, 4)

        @pl.when(g >= 1)
        def _():
            finish(g - 1, 0)

        tiles(4, TILES)

        @pl.when(g >= 2)
        def _():
            finish(g - 2, 2)

        dall[:, kcols] = dk[...].astype(jnp.bfloat16)
        dall[:, vcols] = dv[...].astype(jnp.bfloat16)
        mine = pl.ds(OWN, OWN_N)
        part[g, 0] = (mm(xt[:, mine], dall[mine, cols]) * scale).astype(jnp.bfloat16)
        part[g, 1] = (mm(xt[...], dall[:, kcols]) * scale).astype(jnp.bfloat16)
        part[g, 2] = (mm(xt[...], dall[:, vcols]) * scale).astype(jnp.bfloat16)
        begin(g, 0)

        @pl.when(g >= 1)
        def _():
            finish(g - 1, 1)

        @pl.when(g >= 2)
        def _():
            finish(g - 2, 3)

    @pl.loop(0, QUADS)
    def _(b):
        cols = pl.ds(pl.multiple_of(b * WIDTH, WIDTH), WIDTH)
        rows = jnp.concatenate([dall[ABOVE:OWN, D:], dall[BELOW:, D:]], axis=0)
        value = mm(rows, w[cols, D:], NT).astype(jnp.bfloat16)
        lat_out[:, cols] = value[: 2 * BAND]
        edge[:, cols] = mm(side[...], value[2 * BAND :], TN).astype(jnp.bfloat16)

    give_back(True)
    finish(3, 0)
    finish(2, 2)

    @pl.loop(0, QUADS)
    def _(b):
        cols = pl.ds(pl.multiple_of(b * WIDTH, WIDTH), WIDTH)
        own_grad[:, cols] = mm(dall[OWN:BELOW, :], w[cols, :], NT)

    finish(2, 3)
    finish(3, 1)
    give_back(False)

    @pl.loop(0, QUADS)
    def _(b):
        cols = pl.ds(pl.multiple_of(b * WIDTH, WIDTH), WIDTH)
        value = own_grad[:, cols] + mm(pack[...], back[:, cols], TN)
        gi[:, cols] = value.astype(jnp.bfloat16)
        gi[:BAND, cols] = (value[:BAND] + lat_in[:BAND, cols].astype(jnp.float32)).astype(jnp.bfloat16)
        gi[OWN_N - BAND :, cols] = (
            value[OWN_N - BAND :] + lat_in[BAND:, cols].astype(jnp.float32)
        ).astype(jnp.bfloat16)

    finish(3, 2)
    finish(3, 3)


def fused(x, go, w, scale):
    bf, f32 = jnp.bfloat16, jnp.float32
    kinds = (bf, bf, bf, f32)
    pack, side = packing()
    scratch = [
        pltpu.VMEM((OWN_N, D), bf),
        pltpu.VMEM((D, 3 * D), bf),
        pltpu.VMEM((SIDES, PACKED), bf),
        pltpu.VMEM((TOKENS, D), bf),
        pltpu.VMEM((PACKED, D), bf),
        pltpu.VMEM((PACKED, D), bf),
        pltpu.VMEM((OWN_N, D), bf),
        pltpu.VMEM((TOKENS, D), bf),
        pltpu.VMEM((TOKENS, D), bf),
        pltpu.VMEM((TOKENS, 3 * D), bf),
        pltpu.VMEM((TOKENS, WIDTH), f32),
        pltpu.VMEM((TOKENS, WIDTH), f32),
        pltpu.VMEM((TILES, KEYS, WIDTH), f32),
        pltpu.VMEM((WIDTH, WIDTH), bf),
        pltpu.VMEM((D, TOKENS), bf),
        pltpu.VMEM((QUADS, 3, D, WIDTH), bf),
    ]
    scratch += [pltpu.VMEM((QUADS, 3, LEFT[s - 1], WIDTH), kinds[s]) for s in range(1, 4)]
    scratch += [pltpu.VMEM((QUADS, STAGES[s] - 1, 3, LEFT[s], WIDTH), kinds[s]) for s in range(4)]
    scratch += [
        pltpu.VMEM((PACKED, D), bf),
        pltpu.VMEM((PACKED, D), bf),
        pltpu.VMEM((2 * BAND, D), bf),
        pltpu.VMEM((2 * BAND, D), bf),
        pltpu.VMEM((OWN_N, D), f32),
        pltpu.SemaphoreType.DMA((3,)),
        pltpu.SemaphoreType.DMA((QUADS, 4, 3)),
        pltpu.SemaphoreType.DMA((QUADS, 4, 3)),
        pltpu.SemaphoreType.DMA((8,)),
        pltpu.SemaphoreType.DMA((8,)),
        pltpu.SemaphoreType.DMA((8,)),
        pltpu.SemaphoreType.DMA((8,)),
    ]
    vmem = pl.BlockSpec(memory_space=pltpu.VMEM)
    anywhere = pl.BlockSpec(memory_space=pl.ANY)
    return pl.pallas_call(
        functools.partial(fused_kernel, scale),
        out_shape=[
            jax.ShapeDtypeStruct((OWN_N, D), bf),
            jax.ShapeDtypeStruct((8, 3 * D), f32),
        ],
        in_specs=[vmem, vmem, anywhere, anywhere, anywhere],
        out_specs=[vmem, vmem],
        scratch_shapes=scratch,
        compiler_params=pltpu.CompilerParams(
            collective_id=0, has_side_effects=True, vmem_limit_bytes=61 * 2**20
        ),
        name="attention_backward",
    )(x, pack, go, w, side)


def body(inputs, grad_out, w_qkv):
    scale = float(2 * 128 * 256) ** -0.5
    gi, gw = fused(inputs.reshape(OWN_N, D), grad_out.reshape(OWN_N, D), w_qkv, scale)
    return gi.reshape(inputs.shape), gw


def solution(mesh):
    in_specs = (P("dp", "lat", "lon", None), P("dp", "lat", "lon", None), P())
    out_specs = (P("dp", "lat", "lon", None), P(("dp", "lat", "lon"), None))
    return jax.shard_map(body, mesh=mesh, in_specs=in_specs, out_specs=out_specs, check_vma=False)
```

time: 189 us -> 115 us (0.61)
  waiting for transfers between devices: 27.5 us -> 0 us
  starting transfers between devices: 21.2 us -> 0 us
  Pallas kernels: 120 us -> 110 us
  other arithmetic: 7.64 us -> 0 us
  local copies, waits for them, and re-layouts: 11.4 us -> 3.84 us
    ppermute x8 -> x0, waiting for transfers between devices: 27.5 us -> none  [shifted(): return lax.ppermute(block, axis, route)]
    ppermute x8 -> x0, starting transfers between devices: 21.2 us -> none  [shifted(): return lax.ppermute(block, axis, route)]
    pallas_call x2 -> x1, Pallas kernels: 120 us -> 110 us  [fused(): pl.pallas_call(functools.partial(fused_kernel, scale), out_shape=[jax.Sha...]
    concatenate x3 -> x0, other arithmetic: 4.1 us -> none  [the longest x1 3.18 us: extended(): return jnp.concatenate([lead, tall.reshape(-1, D), sides, end], axis=0)]
    slice x8 -> x0, local copies, waits for them, and re-layouts: 4.05 us -> none  [the longest x1 1.77 us: given_back(): gi[SPLIT:SPLIT + (LAT_DEV + SIDE) * SIDE].reshape(LAT_DEV + SIDE, SIDE, D)]
    reshape x2 -> x0, local copies, waits for them, and re-layouts: 2.02 us -> none  [the longest x1 1.32 us: extended(): sides = jnp.concatenate([left, right], axis=1).reshape(-1, D)]
    another operation x1 -> x0, other arithmetic: 1.99 us -> none
    unnamed x8 -> x2, local copies, waits for them, and re-layouts: 3.37 us -> 3.84 us
  transfers between devices with their start and end apart: 8 -> 0, of which waited for: 5 -> 0; matrix products, arithmetic and copies ran while one was open for 1% -> 0% of each run, Pallas kernels for 31% -> 0%
where the time goes in v2:
time: 115 us; the launch traced here: 114 us
  Pallas kernels  110 us (96%)
  local copies, waits for them, and re-layouts  3.84 us (3%)
    pallas_call x1, Pallas kernels, fused(): pl.pallas_call(functools.partial(fused_kernel, scale), out_shape=[jax.Sha...  110 us
    unnamed x2, local copies, waits for them, and re-layouts  3.84 us

profile of v2, /device:TPU:0, one launch (start us, length us, event | category | flops | bytes accessed | tf_op | source)
XLA Modules:
  0.0 114.4 jit_solution(11420220886096074286)
XLA Ops:
  0.6 109.9 %attention_backward.1 = (bf16[512,1024]{1,0:T(8,128)(2,1)}, f32[8,3072]{1,0:T(8,128)}) custom-call(bf16[512,1024]{1,0:T(8,128)(2,1)} %bitcast.4, bf16[576,512]{1,0:T(8,128)(2,1)} %constant.4.clone.pack, bf16[512,1024]{1,0:T(8,128)(2,1)} %bitcast.5, bf16[1024,3072]{1,0:T(8,128)(2,1)} %w_hbm.1, bf16[544,576]{1,0:T(8,128)(2,1)} %constant.5.clone.side_hbm), custom_call_target="tpu_custom_call" | custom-call | tf_op jit(solution)/shard_map/attention_backward/pallas_call | solution.py:471
  110.6 2.3 %copy.9 = bf16[1,32,16,1024]{3,2,1,0:T(8,128)(2,1)} copy(bf16[1,32,16,1024]{3,2,1,0:T(8,128)(2,1)} %bitcast.3) | data formatting | bytes 2097152
  112.9 1.5 %copy.10 = f32[8,3072]{1,0:T(8,128)} copy(f32[8,3072]{1,0:T(8,128)} %get-tuple-element.9) | data formatting | bytes 196608

commit v3 on v2

--- a/solution.py
+++ b/solution.py
@@ -72,12 +72,13 @@
     own = pl.ds(t * QUERIES, QUERIES)
     ka = pl.ds(pl.multiple_of(PAD_ROWS * LON_DEV + top * QUERIES, 32), KEYS_A)
     kb = pl.ds(pl.multiple_of(SPLIT + top * ROW_T * SIDE, 16), KEYS_B)
+    kind = min(t, 2) if t < TILES - 2 else t - TILES + 5
     same_head = same[...]
     bq = spread(q[own, cols], same_head)
     bg = spread(go[own, cols], same_head)
     keys_a, keys_b = kv[ka, cols], kv[kb, cols]
-    sa = mm(keys_a, bq, NT) + bias[t, :KEYS_A, :]
-    sb = mm(keys_b, bq, NT) + bias[t, KEYS_A:, :]
+    sa = mm(keys_a, bq, NT) + bias[kind, :KEYS_A, :]
+    sb = mm(keys_b, bq, NT) + bias[kind, KEYS_A:, :]
     peak = jnp.maximum(jnp.max(sa, axis=0, keepdims=True), jnp.max(sb, axis=0, keepdims=True))
     pa = jnp.exp(sa - peak)
     pb = jnp.exp(sb - peak)
@@ -105,19 +106,6 @@
     dq[rows, cols] = (total * HEAD**-0.5).astype(jnp.bfloat16)
 
 
-def feature_order(block):
-    row = lax.broadcasted_iota(jnp.int32, (256, D), 0) + block * 256
-    col = lax.broadcasted_iota(jnp.int32, (256, D), 1)
-    r = row & 7
-    xlo = (row >> 3) & 1
-    xhi = (row >> 4) & 1
-    y = (row >> 5) & 3
-    z = (row >> 7) & 3
-    core = row >> 9
-    source = (((((xlo * 4 + y) * 2 + xhi) * 4 + z) * 2 + core) << 3) + r
-    return jnp.where(col == source, 1.0, 0.0).astype(jnp.bfloat16)
-
-
 STAGES = (2, 4, 4, 4)
 LEFT = (512, 128, 32, 8)
 
@@ -131,21 +119,40 @@
     return (xlo, y, xhi * 8 + z * 2 + core)
 
 
-def peers(stage):
+ORDERS = ("zyx", "yxz", "xzy")
+
+
+def along(axis):
     xlo, y, xhi, z, core = place()
-    if stage == 0:
-        return core, [(1 - core, device(xlo, y, xhi, z, 1 - core))]
-    me = (None, z, y, xhi * 2 + xlo)[stage]
+    me = {"x": xhi * 2 + xlo, "y": y, "z": z}[axis]
     others = []
     for step in (1, 3, 2):
         to = (me + step) & 3
-        if stage == 1:
+        if axis == "z":
             others.append((to, device(xlo, y, xhi, to, core)))
-        elif stage == 2:
+        elif axis == "y":
             others.append((to, device(xlo, to, xhi, z, core)))
         else:
             others.append((to, device(to & 1, y, to >> 1, z, core)))
     return me, others
+
+
+def peers(stage, i):
+    if stage == 0:
+        xlo, y, xhi, z, core = place()
+        return core, [(1 - core, device(xlo, y, xhi, z, 1 - core))]
+    return along(ORDERS[i][stage - 1])
+
+
+def by_owner(value, order):
+    blocks = []
+    for core in range(2):
+        for n in range(64):
+            at = dict(zip(order, (n >> 4, (n >> 2) & 3, n & 3)))
+            xlo, xhi = at["x"] & 1, at["x"] >> 1
+            start = ((((xlo * 4 + at["y"]) * 2 + xhi) * 4 + at["z"]) * 2 + core) * 8
+            blocks.append(value[start : start + 8])
+    return jnp.concatenate(blocks, axis=0)
 
 
 SLOTS = ((0, 192, 0, -1), (192, 192, 0, 1), (384, 48, -1, -1), (432, 48, -1, 1), (480, 48, 1, -1), (528, 48, 1, 1))
@@ -212,8 +219,8 @@
 
     barrier = pltpu.get_barrier_semaphore()
     count = 0
-    for stage in range(4):
-        for _, dev in peers(stage)[1]:
+    for others in (peers(0, 0)[1], along("x")[1], along("y")[1], along("z")[1]):
+        for _, dev in others:
             pl.semaphore_signal(barrier, inc=1, device_id=dev, device_id_type=MESH)
             count += 1
     for dy, dx in moves:
@@ -294,11 +301,12 @@
         k[OWN : OWN + OWN_N, cols] = mm(x[...], w[:, kcols]).astype(jnp.bfloat16)
         v[OWN : OWN + OWN_N, cols] = mm(x[...], w[:, vcols]).astype(jnp.bfloat16)
 
-    @pl.loop(0, TILES)
-    def _(t):
+    @pl.loop(0, 5)
+    def _(n):
+        t = n + (TILES - 5) * (n >= 3).astype(jnp.int32)
         top = key_tile(t, first_band, last_band)
-        bias[t, :KEYS_A, :] = window_bias(t, top, KEYS_A, False, band_start, total_rows)
-        bias[t, KEYS_A:, :] = window_bias(t, top, KEYS_B, True, band_start, total_rows)
+        bias[n, :KEYS_A, :] = window_bias(t, top, KEYS_A, False, band_start, total_rows)
+        bias[n, KEYS_A:, :] = window_bias(t, top, KEYS_B, True, band_start, total_rows)
 
     loads[1].wait()
     loads[2].wait()
@@ -316,41 +324,41 @@
             into[:OWN, cols] = value[:OWN]
             into[BELOW:, cols] = value[OWN:]
         rows = pl.ds(pl.multiple_of(b * 256, 256), 256)
-        xt[rows, :] = mm(feature_order(b), xe[...], NT).astype(jnp.bfloat16)
-
-    def copies(c, stage):
+        xt[rows, :] = xe[:, rows].T
+
+    def copies(c, stage, i):
         return [
             pltpu.make_async_remote_copy(
-                src_ref=held[stage].at[c, :, pl.ds(to * LEFT[stage], LEFT[stage]), :],
-                dst_ref=got[stage].at[c, n],
-                send_sem=send.at[c, stage, n],
-                recv_sem=recv.at[c, stage, n],
+                src_ref=held[stage].at[c, i, pl.ds(to * LEFT[stage], LEFT[stage]), :],
+                dst_ref=got[stage].at[c, i, n],
+                send_sem=send.at[c, stage, i, n],
+                recv_sem=recv.at[c, stage, i, n],
                 device_id=dev,
                 device_id_type=MESH,
             )
-            for n, (to, dev) in enumerate(peers(stage)[1])
+            for n, (to, dev) in enumerate(peers(stage, i)[1])
         ]
 
-    def begin(c, stage):
-        for copy in copies(c, stage):
+    def begin(c, stage, i):
+        for copy in copies(c, stage, i):
             copy.start()
 
     def finish(c, stage):
-        for copy in copies(c, stage):
-            copy.wait()
-        me, others = peers(stage)
-        rows = pl.ds(pl.multiple_of(me * LEFT[stage], LEFT[stage]), LEFT[stage])
         for i in range(3):
+            for copy in copies(c, stage, i):
+                copy.wait()
+            me, others = peers(stage, i)
+            rows = pl.ds(pl.multiple_of(me * LEFT[stage], LEFT[stage]), LEFT[stage])
             value = held[stage][c, i, rows, :].astype(jnp.float32)
             for n in range(len(others)):
-                value = value + got[stage][c, n, i].astype(jnp.float32)
+                value = value + got[stage][c, i, n].astype(jnp.float32)
             if stage == 3:
                 at = i * D + c * WIDTH
-                gw[:, pl.ds(at if isinstance(at, int) else pl.multiple_of(at, WIDTH), WIDTH)] = value
+                at = at if isinstance(at, int) else pl.multiple_of(at, WIDTH)
+                gw[:, pl.ds(at, WIDTH)] = value
             else:
                 held[stage + 1][c, i] = value.astype(held[stage + 1].dtype)
-        if stage < 3:
-            begin(c, stage + 1)
+                begin(c, stage + 1, i)
 
     @pl.loop(0, QUADS)
     def _(g):
@@ -380,10 +388,10 @@
         dall[:, kcols] = dk[...].astype(jnp.bfloat16)
         dall[:, vcols] = dv[...].astype(jnp.bfloat16)
         mine = pl.ds(OWN, OWN_N)
-        part[g, 0] = (mm(xt[:, mine], dall[mine, cols]) * scale).astype(jnp.bfloat16)
-        part[g, 1] = (mm(xt[...], dall[:, kcols]) * scale).astype(jnp.bfloat16)
-        part[g, 2] = (mm(xt[...], dall[:, vcols]) * scale).astype(jnp.bfloat16)
-        begin(g, 0)
+        for i, tokens, wide in ((0, mine, cols), (1, slice(None), kcols), (2, slice(None), vcols)):
+            value = mm(xt[:, tokens], dall[tokens, wide]) * scale
+            part[g, i] = by_owner(value, ORDERS[i]).astype(jnp.bfloat16)
+            begin(g, 0, i)
 
         @pl.when(g >= 1)
         def _():
@@ -445,13 +453,13 @@
         pltpu.VMEM((TOKENS, 3 * D), bf),
         pltpu.VMEM((TOKENS, WIDTH), f32),
         pltpu.VMEM((TOKENS, WIDTH), f32),
-        pltpu.VMEM((TILES, KEYS, WIDTH), f32),
+        pltpu.VMEM((5, KEYS, WIDTH), f32),
         pltpu.VMEM((WIDTH, WIDTH), bf),
         pltpu.VMEM((D, TOKENS), bf),
         pltpu.VMEM((QUADS, 3, D, WIDTH), bf),
     ]
     scratch += [pltpu.VMEM((QUADS, 3, LEFT[s - 1], WIDTH), kinds[s]) for s in range(1, 4)]
-    scratch += [pltpu.VMEM((QUADS, STAGES[s] - 1, 3, LEFT[s], WIDTH), kinds[s]) for s in range(4)]
+    scratch += [pltpu.VMEM((QUADS, 3, STAGES[s] - 1, LEFT[s], WIDTH), kinds[s]) for s in range(4)]
     scratch += [
         pltpu.VMEM((PACKED, D), bf),
         pltpu.VMEM((PACKED, D), bf),
@@ -459,8 +467,8 @@
         pltpu.VMEM((2 * BAND, D), bf),
         pltpu.VMEM((OWN_N, D), f32),
         pltpu.SemaphoreType.DMA((3,)),
-        pltpu.SemaphoreType.DMA((QUADS, 4, 3)),
-        pltpu.SemaphoreType.DMA((QUADS, 4, 3)),
+        pltpu.SemaphoreType.DMA((QUADS, 4, 3, 3)),
+        pltpu.SemaphoreType.DMA((QUADS, 4, 3, 3)),
         pltpu.SemaphoreType.DMA((8,)),
         pltpu.SemaphoreType.DMA((8,)),
         pltpu.SemaphoreType.DMA((8,)),

time: 115 us -> 100 us (0.87)
  Pallas kernels: 110 us -> 95.4 us
    pallas_call x1, Pallas kernels: 110 us -> 95.4 us  [fused(): pl.pallas_call(functools.partial(fused_kernel, scale), out_shape=[jax.Sha...]
where the time goes in v3:
time: 100 us; the launch traced here: 99.8 us
  Pallas kernels  95.4 us (95%)
  local copies, waits for them, and re-layouts  3.84 us (4%)
    pallas_call x1, Pallas kernels, fused(): pl.pallas_call(functools.partial(fused_kernel, scale), out_shape=[jax.Sha...  95.4 us
    unnamed x2, local copies, waits for them, and re-layouts  3.84 us

profile of v3, /device:TPU:0, one launch (start us, length us, event | category | flops | bytes accessed | tf_op | source)
XLA Modules:
  0.0 99.8 jit_solution(6647339030387874603)
XLA Ops:
  0.6 95.4 %attention_backward.1 = (bf16[512,1024]{1,0:T(8,128)(2,1)}, f32[8,3072]{1,0:T(8,128)}) custom-call(bf16[512,1024]{1,0:T(8,128)(2,1)} %bitcast.4, bf16[576,512]{1,0:T(8,128)(2,1)} %constant.4.clone.pack, bf16[512,1024]{1,0:T(8,128)(2,1)} %bitcast.5, bf16[1024,3072]{1,0:T(8,128)(2,1)} %w_hbm.1, bf16[544,576]{1,0:T(8,128)(2,1)} %constant.5.clone.side_hbm), custom_call_target="tpu_custom_call" | custom-call | tf_op jit(solution)/shard_map/attention_backward/pallas_call | solution.py:479
  96.0 2.3 %copy.9 = bf16[1,32,16,1024]{3,2,1,0:T(8,128)(2,1)} copy(bf16[1,32,16,1024]{3,2,1,0:T(8,128)(2,1)} %bitcast.3) | data formatting | bytes 2097152
  98.3 1.5 %copy.10 = f32[8,3072]{1,0:T(8,128)} copy(f32[8,3072]{1,0:T(8,128)} %get-tuple-element.9) | data formatting | bytes 196608

commit v4 on v3

--- a/solution.py
+++ b/solution.py
@@ -178,14 +178,14 @@
                 row = r + (MARGIN if dy == 0 else 0 if dy < 0 else LAT_DEV + MARGIN)
                 col = c + (MARGIN if dx > 0 else 0)
                 side[row * SIDE + col, start + r * MARGIN + c] = 1
-    return jnp.asarray(pack, jnp.bfloat16), jnp.asarray(side, jnp.bfloat16)
+    return [jnp.asarray(m, jnp.bfloat16) for m in (pack, side, pack.T, side.T)]
 
 
 def fused_kernel(
-    scale, x, pack, go_hbm, w_hbm, side_hbm, gi, gw,
-    go, w, side, xe, packed, halo, q, k, v, dall, dk, dv, bias, same, xt,
+    scale, x, pack, go_hbm, w_hbm, side_hbm, unpack_hbm, unside_hbm, gi, gw,
+    go, w, side, unpack, unside, xe, packed, halo, q, k, v, dall, dk, dv, bias, same, xt,
     part, held1, held2, held3, got0, got1, got2, got3,
-    edge, back, lat_out, lat_in, own_grad,
+    back, lat_out, lat_in, own_grad,
     load, send, recv, halo_send, halo_recv, back_send, back_recv,
 ):
     dp, lat, lon = lax.axis_index("dp"), lax.axis_index("lat"), lax.axis_index("lon")
@@ -200,6 +200,8 @@
         pltpu.make_async_copy(w_hbm, w, load.at[0]),
         pltpu.make_async_copy(go_hbm, go, load.at[1]),
         pltpu.make_async_copy(side_hbm, side, load.at[2]),
+        pltpu.make_async_copy(unpack_hbm, unpack, load.at[3]),
+        pltpu.make_async_copy(unside_hbm, unside, load.at[4]),
     ]
     for copy in loads:
         copy.start()
@@ -266,7 +268,7 @@
 
     def give_back(sending):
         exchange(
-            edge, back, lat_out.at[pl.ds(0, BAND), :], lat_out.at[pl.ds(BAND, BAND), :],
+            packed, back, lat_out.at[pl.ds(0, BAND), :], lat_out.at[pl.ds(BAND, BAND), :],
             lat_in.at[pl.ds(0, BAND), :], lat_in.at[pl.ds(BAND, BAND), :],
             back_send, back_recv, sending,
         )
@@ -308,8 +310,8 @@
         bias[n, :KEYS_A, :] = window_bias(t, top, KEYS_A, False, band_start, total_rows)
         bias[n, KEYS_A:, :] = window_bias(t, top, KEYS_B, True, band_start, total_rows)
 
-    loads[1].wait()
-    loads[2].wait()
+    for copy in loads[1:]:
+        copy.wait()
     halo_exchange(False)
     xe[SPLIT:, :] = mm(side[...], halo[...]).astype(jnp.bfloat16)
 
@@ -373,13 +375,13 @@
                 top = key_tile(t, first_band, last_band)
                 attend(t, top, cols, q, k, v, go, bias, same, dk, dv, dall)
 
-        tiles(0, 4)
+        tiles(0, 5)
 
         @pl.when(g >= 1)
         def _():
             finish(g - 1, 0)
 
-        tiles(4, TILES)
+        tiles(5, TILES)
 
         @pl.when(g >= 2)
         def _():
@@ -401,49 +403,71 @@
         def _():
             finish(g - 2, 3)
 
-    @pl.loop(0, QUADS)
-    def _(b):
-        cols = pl.ds(pl.multiple_of(b * WIDTH, WIDTH), WIDTH)
+    def edge_grads(b):
+        cols = pl.ds(b * WIDTH, WIDTH)
         rows = jnp.concatenate([dall[ABOVE:OWN, D:], dall[BELOW:, D:]], axis=0)
         value = mm(rows, w[cols, D:], NT).astype(jnp.bfloat16)
         lat_out[:, cols] = value[: 2 * BAND]
-        edge[:, cols] = mm(side[...], value[2 * BAND :], TN).astype(jnp.bfloat16)
-
-    give_back(True)
+        packed[:, cols] = mm(unside[...], value[2 * BAND :]).astype(jnp.bfloat16)
+
+    def own_grads(b):
+        cols = pl.ds(b * WIDTH, WIDTH)
+        own_grad[:, cols] = mm(dall[OWN:BELOW, :], w[cols, :], NT)
+
+    edge_grads(0)
+    edge_grads(1)
     finish(3, 0)
     finish(2, 2)
-
-    @pl.loop(0, QUADS)
-    def _(b):
-        cols = pl.ds(pl.multiple_of(b * WIDTH, WIDTH), WIDTH)
-        own_grad[:, cols] = mm(dall[OWN:BELOW, :], w[cols, :], NT)
-
+    edge_grads(2)
+    edge_grads(3)
+    give_back(True)
+    finish(3, 1)
+    own_grads(0)
+    own_grads(1)
+    finish(3, 2)
+    own_grads(2)
+    own_grads(3)
     finish(2, 3)
-    finish(3, 1)
     give_back(False)
 
-    @pl.loop(0, QUADS)
-    def _(b):
-        cols = pl.ds(pl.multiple_of(b * WIDTH, WIDTH), WIDTH)
-        value = own_grad[:, cols] + mm(pack[...], back[:, cols], TN)
-        gi[:, cols] = value.astype(jnp.bfloat16)
+    for b in range(QUADS):
+        cols = pl.ds(b * WIDTH, WIDTH)
+        value = own_grad[:, cols] + mm(unpack[...], back[:, cols])
+        gi[BAND : OWN_N - BAND, cols] = value[BAND : OWN_N - BAND].astype(jnp.bfloat16)
         gi[:BAND, cols] = (value[:BAND] + lat_in[:BAND, cols].astype(jnp.float32)).astype(jnp.bfloat16)
         gi[OWN_N - BAND :, cols] = (
             value[OWN_N - BAND :] + lat_in[BAND:, cols].astype(jnp.float32)
         ).astype(jnp.bfloat16)
 
-    finish(3, 2)
     finish(3, 3)
+
+
+def copy_kernel(gi_in, gw_in, gi, gw):
+    gi[...] = gi_in[...]
+    gw[...] = gw_in[...]
+
+
+def handed_over(gi, gw):
+    vmem = pl.BlockSpec(memory_space=pltpu.VMEM)
+    return pl.pallas_call(
+        copy_kernel,
+        out_shape=[jax.ShapeDtypeStruct(t.shape, t.dtype) for t in (gi, gw)],
+        in_specs=[vmem] * 2,
+        out_specs=[vmem] * 2,
+        name="hand_over",
+    )(gi, gw)
 
 
 def fused(x, go, w, scale):
     bf, f32 = jnp.bfloat16, jnp.float32
     kinds = (bf, bf, bf, f32)
-    pack, side = packing()
+    pack, side, unpack, unside = packing()
     scratch = [
         pltpu.VMEM((OWN_N, D), bf),
         pltpu.VMEM((D, 3 * D), bf),
         pltpu.VMEM((SIDES, PACKED), bf),
+        pltpu.VMEM((OWN_N, PACKED), bf),
+        pltpu.VMEM((PACKED, SIDES), bf),
         pltpu.VMEM((TOKENS, D), bf),
         pltpu.VMEM((PACKED, D), bf),
         pltpu.VMEM((PACKED, D), bf),
@@ -462,11 +486,10 @@
     scratch += [pltpu.VMEM((QUADS, 3, STAGES[s] - 1, LEFT[s], WIDTH), kinds[s]) for s in range(4)]
     scratch += [
         pltpu.VMEM((PACKED, D), bf),
-        pltpu.VMEM((PACKED, D), bf),
         pltpu.VMEM((2 * BAND, D), bf),
         pltpu.VMEM((2 * BAND, D), bf),
         pltpu.VMEM((OWN_N, D), f32),
-        pltpu.SemaphoreType.DMA((3,)),
+        pltpu.SemaphoreType.DMA((5,)),
         pltpu.SemaphoreType.DMA((QUADS, 4, 3, 3)),
         pltpu.SemaphoreType.DMA((QUADS, 4, 3, 3)),
         pltpu.SemaphoreType.DMA((8,)),
@@ -482,19 +505,20 @@
             jax.ShapeDtypeStruct((OWN_N, D), bf),
             jax.ShapeDtypeStruct((8, 3 * D), f32),
         ],
-        in_specs=[vmem, vmem, anywhere, anywhere, anywhere],
+        in_specs=[vmem, vmem] + [anywhere] * 5,
         out_specs=[vmem, vmem],
         scratch_shapes=scratch,
         compiler_params=pltpu.CompilerParams(
             collective_id=0, has_side_effects=True, vmem_limit_bytes=61 * 2**20
         ),
         name="attention_backward",
-    )(x, pack, go, w, side)
+    )(x, pack, go, w, side, unpack, unside)
 
 
 def body(inputs, grad_out, w_qkv):
     scale = float(2 * 128 * 256) ** -0.5
     gi, gw = fused(inputs.reshape(OWN_N, D), grad_out.reshape(OWN_N, D), w_qkv, scale)
+    gi, gw = handed_over(gi, gw)
     return gi.reshape(inputs.shape), gw
 
 

time: 100 us -> 94.6 us (0.946)
  local copies, waits for them, and re-layouts: 3.84 us -> 0 us
  Pallas kernels: 95.4 us -> 93.4 us
    pallas_call x1, Pallas kernels: 95.4 us -> 91.1 us  [fused(): pl.pallas_call(functools.partial(fused_kernel, scale), out_shape=[jax.Sha...]
    unnamed x2 -> x0, local copies, waits for them, and re-layouts: 3.84 us -> none
    pallas_call x0 -> x1, Pallas kernels: none -> 2.28 us  [handed_over(): pl.pallas_call(copy_kernel, out_shape=[jax.ShapeDtypeStruct(t.shape, t.dt...]
where the time goes in v4:
time: 94.6 us; the launch traced here: 94.1 us
  Pallas kernels  93.4 us (99%)
    pallas_call x1, Pallas kernels, fused(): pl.pallas_call(functools.partial(fused_kernel, scale), out_shape=[jax.Sha...  91.1 us
    pallas_call x1, Pallas kernels, handed_over(): pl.pallas_call(copy_kernel, out_shape=[jax.ShapeDtypeStruct(t.shape, t.dt...  2.28 us

profile of v4, /device:TPU:0, one launch (start us, length us, event | category | flops | bytes accessed | tf_op | source)
XLA Modules:
  0.0 94.1 jit_solution(8463356799229496127)
XLA Ops:
  0.6 91.1 %attention_backward.1 = (bf16[512,1024]{1,0:T(8,128)(2,1)}, f32[8,3072]{1,0:T(8,128)}) custom-call(bf16[512,1024]{1,0:T(8,128)(2,1)} %bitcast.3, bf16[576,512]{1,0:T(8,128)(2,1)} %constant.8.clone.pack, bf16[512,1024]{1,0:T(8,128)(2,1)} %bitcast.4, bf16[1024,3072]{1,0:T(8,128)(2,1)} %w_hbm.1, bf16[544,576]{1,0:T(8,128)(2,1)} %constant.9.clone.side_hbm, ...), custom_call_target="tpu_custom_call" | custom-call | tf_op jit(solution)/shard_map/attention_backward/pallas_call | solution.py:502
  91.8 2.3 %hand_over.1 = (bf16[512,1024]{1,0:T(8,128)(2,1)}, f32[8,3072]{1,0:T(8,128)}) custom-call(bf16[512,1024]{1,0:T(8,128)(2,1)} %get-tuple-element.6.gi_in, f32[8,3072]{1,0:T(8,128)} %get-tuple-element.7.gw_in), custom_call_target="tpu_custom_call" | custom-call | tf_op jit(solution)/shard_map/hand_over/pallas_call | solution.py:452

commit v5 on v4

--- a/solution.py
+++ b/solution.py
@@ -185,7 +185,7 @@
     scale, x, pack, go_hbm, w_hbm, side_hbm, unpack_hbm, unside_hbm, gi, gw,
     go, w, side, unpack, unside, xe, packed, halo, q, k, v, dall, dk, dv, bias, same, xt,
     part, held1, held2, held3, got0, got1, got2, got3,
-    back, lat_out, lat_in, own_grad,
+    back, lat_out, lat_in, own_grad, early,
     load, send, recv, halo_send, halo_recv, back_send, back_recv,
 ):
     dp, lat, lon = lax.axis_index("dp"), lax.axis_index("lat"), lax.axis_index("lon")
@@ -346,7 +346,7 @@
             copy.start()
 
     def finish(c, stage):
-        for i in range(3):
+        for i in (2, 0, 1):
             for copy in copies(c, stage, i):
                 copy.wait()
             me, others = peers(stage, i)
@@ -362,6 +362,9 @@
                 held[stage + 1][c, i] = value.astype(held[stage + 1].dtype)
                 begin(c, stage + 1, i)
 
+    def edges(a, b):
+        return jnp.concatenate([dall[ABOVE:OWN, a:b], dall[BELOW:, a:b]], axis=0)
+
     @pl.loop(0, QUADS)
     def _(g):
         cols = pl.ds(pl.multiple_of(g * WIDTH, WIDTH), WIDTH)
@@ -375,6 +378,15 @@
                 top = key_tile(t, first_band, last_band)
                 attend(t, top, cols, q, k, v, go, bias, same, dk, dv, dall)
 
+        @pl.when(g == QUADS - 1)
+        def _():
+            @pl.loop(0, QUADS)
+            def _(b):
+                out = pl.ds(pl.multiple_of(b * WIDTH, WIDTH), WIDTH)
+                early[:, out] = mm(edges(D, 2 * D - WIDTH), w[out, D : 2 * D - WIDTH], NT) + mm(
+                    edges(2 * D, 3 * D - WIDTH), w[out, 2 * D : 3 * D - WIDTH], NT
+                )
+
         tiles(0, 5)
 
         @pl.when(g >= 1)
@@ -405,8 +417,10 @@
 
     def edge_grads(b):
         cols = pl.ds(b * WIDTH, WIDTH)
-        rows = jnp.concatenate([dall[ABOVE:OWN, D:], dall[BELOW:, D:]], axis=0)
-        value = mm(rows, w[cols, D:], NT).astype(jnp.bfloat16)
+        late = mm(edges(2 * D - WIDTH, 2 * D), w[cols, 2 * D - WIDTH : 2 * D], NT) + mm(
+            edges(3 * D - WIDTH, 3 * D), w[cols, 3 * D - WIDTH :], NT
+        )
+        value = (early[:, cols] + late).astype(jnp.bfloat16)
         lat_out[:, cols] = value[: 2 * BAND]
         packed[:, cols] = mm(unside[...], value[2 * BAND :]).astype(jnp.bfloat16)
 
@@ -414,19 +428,17 @@
         cols = pl.ds(b * WIDTH, WIDTH)
         own_grad[:, cols] = mm(dall[OWN:BELOW, :], w[cols, :], NT)
 
-    edge_grads(0)
-    edge_grads(1)
+    for b in range(QUADS):
+        edge_grads(b)
     finish(3, 0)
+    give_back(True)
     finish(2, 2)
-    edge_grads(2)
-    edge_grads(3)
-    give_back(True)
-    finish(3, 1)
     own_grads(0)
     own_grads(1)
-    finish(3, 2)
+    finish(3, 1)
     own_grads(2)
     own_grads(3)
+    finish(3, 2)
     finish(2, 3)
     give_back(False)
 
@@ -489,6 +501,7 @@
         pltpu.VMEM((2 * BAND, D), bf),
         pltpu.VMEM((2 * BAND, D), bf),
         pltpu.VMEM((OWN_N, D), f32),
+        pltpu.VMEM((OWN + TOKENS - BELOW - ABOVE, D), f32),
         pltpu.SemaphoreType.DMA((5,)),
         pltpu.SemaphoreType.DMA((QUADS, 4, 3, 3)),
         pltpu.SemaphoreType.DMA((QUADS, 4, 3, 3)),

time: 94.6 us -> 95.2 us (level)
  Pallas kernels: 93.4 us -> 94.4 us
    pallas_call x1, Pallas kernels: 91.1 us -> 92.1 us  [fused(): pl.pallas_call(functools.partial(fused_kernel, scale), out_shape=[jax.Sha...]
where the time goes in v5:
time: 95.2 us; the launch traced here: 95 us
  Pallas kernels  94.4 us (99%)
    pallas_call x1, Pallas kernels, fused(): pl.pallas_call(functools.partial(fused_kernel, scale), out_shape=[jax.Sha...  92.1 us
    pallas_call x1, Pallas kernels, handed_over(): pl.pallas_call(copy_kernel, out_shape=[jax.ShapeDtypeStruct(t.shape, t.dt...  2.28 us

profile of v5, /device:TPU:0, one launch (start us, length us, event | category | flops | bytes accessed | tf_op | source)
XLA Modules:
  0.0 95.0 jit_solution(17893007598614938862)
XLA Ops:
  0.6 92.1 %attention_backward.1 = (bf16[512,1024]{1,0:T(8,128)(2,1)}, f32[8,3072]{1,0:T(8,128)}) custom-call(bf16[512,1024]{1,0:T(8,128)(2,1)} %bitcast.3, bf16[576,512]{1,0:T(8,128)(2,1)} %constant.8.clone.pack, bf16[512,1024]{1,0:T(8,128)(2,1)} %bitcast.4, bf16[1024,3072]{1,0:T(8,128)(2,1)} %w_hbm.1, bf16[544,576]{1,0:T(8,128)(2,1)} %constant.9.clone.side_hbm, ...), custom_call_target="tpu_custom_call" | custom-call | tf_op jit(solution)/shard_map/attention_backward/pallas_call | solution.py:515
  92.8 2.3 %hand_over.1 = (bf16[512,1024]{1,0:T(8,128)(2,1)}, f32[8,3072]{1,0:T(8,128)}) custom-call(bf16[512,1024]{1,0:T(8,128)(2,1)} %get-tuple-element.6.gi_in, f32[8,3072]{1,0:T(8,128)} %get-tuple-element.7.gw_in), custom_call_target="tpu_custom_call" | custom-call | tf_op jit(solution)/shard_map/hand_over/pallas_call | solution.py:464

commit v6 on v4

--- a/solution.py
+++ b/solution.py
@@ -346,7 +346,7 @@
             copy.start()
 
     def finish(c, stage):
-        for i in range(3):
+        for i in (1, 2, 0):
             for copy in copies(c, stage, i):
                 copy.wait()
             me, others = peers(stage, i)
@@ -390,7 +390,7 @@
         dall[:, kcols] = dk[...].astype(jnp.bfloat16)
         dall[:, vcols] = dv[...].astype(jnp.bfloat16)
         mine = pl.ds(OWN, OWN_N)
-        for i, tokens, wide in ((0, mine, cols), (1, slice(None), kcols), (2, slice(None), vcols)):
+        for i, tokens, wide in ((1, slice(None), kcols), (2, slice(None), vcols), (0, mine, cols)):
             value = mm(xt[:, tokens], dall[tokens, wide]) * scale
             part[g, i] = by_owner(value, ORDERS[i]).astype(jnp.bfloat16)
             begin(g, 0, i)

time: 94.6 us -> 94.6 us (level)
  no operation moved by 1% of the time
where the time goes in v6:
time: 94.6 us; the launch traced here: 94 us
  Pallas kernels  93.4 us (99%)
    pallas_call x1, Pallas kernels, fused(): pl.pallas_call(functools.partial(fused_kernel, scale), out_shape=[jax.Sha...  91.1 us
    pallas_call x1, Pallas kernels, handed_over(): pl.pallas_call(copy_kernel, out_shape=[jax.ShapeDtypeStruct(t.shape, t.dt...  2.28 us

profile of v6, /device:TPU:0, one launch (start us, length us, event | category | flops | bytes accessed | tf_op | source)
XLA Modules:
  0.0 94.0 jit_solution(17366344935727427635)
XLA Ops:
  0.6 91.1 %attention_backward.1 = (bf16[512,1024]{1,0:T(8,128)(2,1)}, f32[8,3072]{1,0:T(8,128)}) custom-call(bf16[512,1024]{1,0:T(8,128)(2,1)} %bitcast.3, bf16[576,512]{1,0:T(8,128)(2,1)} %constant.8.clone.pack, bf16[512,1024]{1,0:T(8,128)(2,1)} %bitcast.4, bf16[1024,3072]{1,0:T(8,128)(2,1)} %w_hbm.1, bf16[544,576]{1,0:T(8,128)(2,1)} %constant.9.clone.side_hbm, ...), custom_call_target="tpu_custom_call" | custom-call | tf_op jit(solution)/shard_map/attention_backward/pallas_call | solution.py:502
  91.7 2.3 %hand_over.1 = (bf16[512,1024]{1,0:T(8,128)(2,1)}, f32[8,3072]{1,0:T(8,128)}) custom-call(bf16[512,1024]{1,0:T(8,128)(2,1)} %get-tuple-element.6.gi_in, f32[8,3072]{1,0:T(8,128)} %get-tuple-element.7.gw_in), custom_call_target="tpu_custom_call" | custom-call | tf_op jit(solution)/shard_map/hand_over/pallas_call | solution.py:452
